TPU v7x, 128 devices: a whole 4x4x4 slice. The times are simulated.
128 devices in a mesh: gx: 16 (over z, x), gy: 8 (over y, core).
Axes of the slice: x: 4, y: 4, z: 4, core: 2. Of those that a mesh axis runs over, the one named last changes fastest.
Arguments:
- right_side: float32 [1024, 512, 128], P('gx', 'gy'), may hold values from -150 to 150
- diagonal: float32 [1024, 512, 128], P('gx', 'gy'), may hold values from 0.25 to 2
- sweep_counts: int32 [128], replicated, may hold values from 2 to 12, as said below
- refine_flags: int32 [128, 128], replicated, may hold values 0 or 1
- coarse_inverse: float32 [128, 128], P(('gx', 'gy')), as said below
Outputs:
- solution_field: float32 [1024, 512, 128], P('gx', 'gy')
- residual: float32 [1024, 512, 128], P('gx', 'gy')
Inputs may be any that keep to these rules, and one draw needn't show every extreme that they name: `sweep_counts`: every subdomain makes 2 or more sweeps, and some subdomain makes exactly 12. `coarse_inverse`: symmetric positive definite.
All inputs are finite; a program needn't handle non-finite values.
Results may differ from a plain program's by a relative error of at most 0.019.
Values sent between devices are 32-bit elements; how exact they have to be, the bound alone decides.
A program may use at most 128 MiB of HBM per device.

v0:
```python
import jax
import jax.numpy as jnp
from jax import lax
from jax.sharding import PartitionSpec as P

ITERS = 4


HIGH = lax.Precision.HIGHEST


def with_halo(array, sides, width):
    for axis, dim in sides:
        count, length = (lax.axis_size(axis), array.shape[dim])
        up = [(i, (i + 1) % count) for i in range(count - 1)]
        down = [(j, i) for i, j in up]
        last = lax.slice_in_dim(array, length - width, length, axis=dim)
        first = lax.slice_in_dim(array, 0, width, axis=dim)
        before = lax.ppermute(last, axis, up)
        after = lax.ppermute(first, axis, down)
        array = jnp.concatenate([before, array, after], axis=dim)
    return array


def sine_table(count):
    index = jnp.arange(count, dtype=jnp.float32)
    angle = jnp.pi * (index[:, None] + 1.0) * (index[None, :] + 1.0) / (count + 1.0)
    return jnp.sqrt(2.0 / (count + 1.0)) * jnp.sin(angle)


def eigen_values(count):
    index = jnp.arange(count, dtype=jnp.float32)
    return 2.0 - 2.0 * jnp.cos(jnp.pi * (index + 1.0) / (count + 1.0))


def sweep(rhs, guess, scale):
    zero = jnp.zeros_like(guess[..., :1])
    below = jnp.concatenate([zero, guess[..., :-1]], -1)
    above = jnp.concatenate([guess[..., 1:], zero], -1)
    return (rhs + below + above) / scale


def transform(field, table_x, table_y):
    step_one = jnp.einsum("ai,ijz->ajz", table_x, field, precision=HIGH)
    return jnp.einsum("bj,ajz->abz", table_y, step_one, precision=HIGH)


def operate(field, diagonal):
    padded = with_halo(field, (("gx", 0), ("gy", 1)), 1)
    padded = jnp.pad(padded, ((0, 0), (0, 0), (1, 1)))
    beside = padded[2:, 1:-1, 1:-1] + padded[:-2, 1:-1, 1:-1]
    beside = beside + padded[1:-1, 2:, 1:-1] + padded[1:-1, :-2, 1:-1]
    beside = beside + padded[1:-1, 1:-1, 2:] + padded[1:-1, 1:-1, :-2]
    return (6.0 + diagonal) * field - beside


def precondition(resid, sweep_counts, refine_flags, coarse_row):
    size_x, size_y, cells = resid.shape
    position = lax.axis_index(("gx", "gy"))
    table_x = sine_table(size_x)
    table_y = sine_table(size_y)
    hat = transform(resid, table_x, table_y).reshape(size_x * size_y, cells)
    modal = (eigen_values(size_x)[:, None] + eigen_values(size_y)[None, :]).reshape(
        size_x * size_y, 1
    )
    shifts = 0.5 + 2.5 * refine_flags.astype(jnp.float32)
    scale = modal + 2.0
    scale = scale + lax.dynamic_index_in_dim(shifts, position, 0, keepdims=True)
    count = sweep_counts[position]
    lines = lax.fori_loop(
        0, count, lambda step, guess: sweep(hat, guess, scale), jnp.zeros_like(hat)
    )
    back = transform(lines.reshape(size_x, size_y, cells), table_x, table_y)
    total = jnp.sum(resid).reshape(1)
    sums = lax.all_gather(total, ("gx", "gy"), axis=0, tiled=True)
    coarse = jnp.dot(coarse_row[0], sums, precision=HIGH)
    return back + coarse


def inner_sum(first, second):
    return lax.psum(jnp.sum(first * second), ("gx", "gy"))


def shards(right_side, diagonal, sweep_counts, refine_flags, coarse_inverse):
    solution_field = jnp.zeros_like(right_side)
    residual = right_side
    precond = precondition(residual, sweep_counts, refine_flags, coarse_inverse)
    direction = precond
    gamma = inner_sum(residual, precond)
    for step in range(ITERS):
        image = operate(direction, diagonal)
        alpha = gamma / lax.psum(jnp.sum(direction * image), ("gx", "gy"))
        solution_field = solution_field + alpha * direction
        residual = residual - alpha * image
        if step + 1 < ITERS:
            precond = precondition(residual, sweep_counts, refine_flags, coarse_inverse)
            fresh = inner_sum(residual, precond)
            direction = precond + fresh / gamma * direction
            gamma = fresh
    return (solution_field, residual)


def solution(mesh):
    return jax.shard_map(
        shards,
        mesh=mesh,
        in_specs=(P("gx", "gy", None), P("gx", "gy", None), P(), P(), P(("gx", "gy"), None)),
        out_specs=(P("gx", "gy", None), P("gx", "gy", None)),
        check_vma=False,
    )
```

profile of v0, /device:TPU:1, one launch (start us, length us, event | category | flops | bytes accessed | tf_op | source)
XLA Modules:
  0.0 1101.7 jit_solution(16801006305267590016)
XLA Ops:
  11.8 10.9 while.44
  30.7 98.2 %all-reduce.12 = f32[128]{0:T(128)S(1)} all-reduce(f32[128]{0:T(128)S(1)} %dynamic-update-slice), channel_id=1, replica_groups=mesh['gx'=16,'gy'=8] {'gx','gy'}, use_global_device_ids=true, to_apply=%add.12 | all-reduce | flops 128 | bytes 1024
  129.5 5.6 add_bitcast_fusion
  152.6 5.7 multiply_reduce_fusion.3
  158.4 67.6 %all-reduce.16 = (f32[]{:T(128)}, f32[]{:T(128)}) all-reduce(f32[]{:T(128)} %get-tuple-element.187, f32[]{:T(128)} %get-tuple-element.186), channel_id=1, replica_groups=mesh['gx'=16,'gy'=8] {'gx','gy'}, use_global_device_ids=true, to_apply=%region_4.5 | all-reduce | flops 2 | bytes 16 | tf_op jit(solution)/shard_map/psum | solution.py:81
  238.8 11.0 %while.45 = (s32[]{:T(128)}, f32[4096,128]{1,0:T(8,128)S(1)}, s32[]{:T(128)}, f32[4096,128]{1,0:T(8,128)}, f32[128]{0:T(128)S(1)}, /*index=5*/f32[4096]{0:T(1024)S(1)}, s32[]{:T(128)}) while((s32[]{:T(128)}, f32[4096,128]{1,0:T(8,128)S(1)}, s32[]{:T(128)}, f32[4096,128]{1,0:T(8,128)}, f32[128]{0:T(128)S(1)}, ...), condition=%wide.region_8.9_spmd.clone, body=%wide.region_7.8_spmd.clone.sunk | while | flops 2097154 | bytes 25084520 | solution.py:70
  255.1 93.7 %all-reduce.13 = f32[128]{0:T(128)S(1)} all-reduce(f32[128]{0:T(128)S(1)} %dynamic-update-slice.1), channel_id=1, replica_groups=mesh['gx'=16,'gy'=8] {'gx','gy'}, use_global_device_ids=true, to_apply=%add.13 | all-reduce | flops 128 | bytes 1024
  349.5 8.2 fusion.27
  357.7 62.6 %psum.58 = f32[]{:T(128)} all-reduce(f32[]{:T(128)} %get-tuple-element.275), channel_id=1, replica_groups=mesh['gx'=16,'gy'=8] {'gx','gy'}, use_global_device_ids=true, to_apply=%region_11.12 | all-reduce | flops 1 | bytes 8 | tf_op jit(solution)/shard_map/psum | solution.py:81
  438.1 5.4 select_maximum_fusion.8
  443.6 5.8 multiply_reduce_fusion.2
  449.4 67.0 %psum.59 = f32[]{:T(128)} all-reduce(f32[]{:T(128)} %get-tuple-element.246), channel_id=1, replica_groups=mesh['gx'=16,'gy'=8] {'gx','gy'}, use_global_device_ids=true, to_apply=%region_13.14 | all-reduce | flops 1 | bytes 8 | tf_op jit(solution)/shard_map/psum | solution.py:92
  528.6 11.3 %while.46 = (s32[]{:T(128)}, f32[4096,128]{1,0:T(8,128)S(1)}, s32[]{:T(128)}, f32[4096,128]{1,0:T(8,128)}, f32[128]{0:T(128)S(1)}, /*index=5*/f32[4096]{0:T(1024)S(1)}, s32[]{:T(128)}) while((s32[]{:T(128)}, f32[4096,128]{1,0:T(8,128)S(1)}, s32[]{:T(128)}, f32[4096,128]{1,0:T(8,128)}, f32[128]{0:T(128)S(1)}, ...), condition=%wide.region_15.16_spmd.clone, body=%wide.region_14.15_spmd.clone.sunk | while | flops 2097154 | bytes 25084520 | solution.py:70
  545.2 93.7 %all-reduce.14 = f32[128]{0:T(128)S(1)} all-reduce(f32[128]{0:T(128)S(1)} %dynamic-update-slice.2), channel_id=1, replica_groups=mesh['gx'=16,'gy'=8] {'gx','gy'}, use_global_device_ids=true, to_apply=%add.14 | all-reduce | flops 128 | bytes 1024
  639.5 8.1 fusion.26
  647.6 62.6 %psum.60 = f32[]{:T(128)} all-reduce(f32[]{:T(128)} %get-tuple-element.277), channel_id=1, replica_groups=mesh['gx'=16,'gy'=8] {'gx','gy'}, use_global_device_ids=true, to_apply=%region_18.19 | all-reduce | flops 1 | bytes 8 | tf_op jit(solution)/shard_map/psum | solution.py:81
  732.1 5.9 multiply_reduce_fusion.1
  737.9 66.9 %psum.61 = f32[]{:T(128)} all-reduce(f32[]{:T(128)} %get-tuple-element.242), channel_id=1, replica_groups=mesh['gx'=16,'gy'=8] {'gx','gy'}, use_global_device_ids=true, to_apply=%region_20.21 | all-reduce | flops 1 | bytes 8 | tf_op jit(solution)/shard_map/psum | solution.py:92
  817.1 11.1 %while.47 = (s32[]{:T(128)}, f32[4096,128]{1,0:T(8,128)S(1)}, s32[]{:T(128)}, f32[4096,128]{1,0:T(8,128)}, f32[128]{0:T(128)S(1)}, /*index=5*/f32[4096]{0:T(1024)S(1)}, s32[]{:T(128)}) while((s32[]{:T(128)}, f32[4096,128]{1,0:T(8,128)S(1)}, s32[]{:T(128)}, f32[4096,128]{1,0:T(8,128)}, f32[128]{0:T(128)S(1)}, ...), condition=%wide.region_22.23_spmd.clone, body=%wide.region_21.22_spmd.clone.sunk | while | flops 2097154 | bytes 25084520 | solution.py:70
  833.4 93.8 %all-reduce.15 = f32[128]{0:T(128)S(1)} all-reduce(f32[128]{0:T(128)S(1)} %dynamic-update-slice.3), channel_id=1, replica_groups=mesh['gx'=16,'gy'=8] {'gx','gy'}, use_global_device_ids=true, to_apply=%add.15 | all-reduce | flops 128 | bytes 1024
  927.8 8.1 fusion.25
  935.9 62.5 %psum.62 = f32[]{:T(128)} all-reduce(f32[]{:T(128)} %get-tuple-element.279), channel_id=1, replica_groups=mesh['gx'=16,'gy'=8] {'gx','gy'}, use_global_device_ids=true, to_apply=%region_25.26 | all-reduce | flops 1 | bytes 8 | tf_op jit(solution)/shard_map/psum | solution.py:81
  1019.9 5.8 multiply_reduce_fusion
  1025.7 67.2 %psum.63 = f32[]{:T(128)} all-reduce(f32[]{:T(128)} %get-tuple-element.238), channel_id=1, replica_groups=mesh['gx'=16,'gy'=8] {'gx','gy'}, use_global_device_ids=true, to_apply=%region_27.28 | all-reduce | flops 1 | bytes 8 | tf_op jit(solution)/shard_map/psum | solution.py:92
  (180 shorter events, 186.4 us)
Async XLA Ops:
  27.2 101.7 %copy-start.26 = (f32[1,128]{1,0:T(1,128)S(1)}, f32[1,128]{1,0:T(1,128)}, u32[]{:S(2)}) copy-start(f32[1,128]{1,0:T(1,128)} %param.17) | copy-start | bytes 1540
  135.1 5.3 collective-permute-start
  136.4 5.0 collective-permute-start.1
  141.5 6.5 collective-permute-start.2
  145.1 3.7 collective-permute-start.3
  349.4 72.1 %copy-start.1 = (f32[64,64,128]{2,1,0:T(8,128)S(1)}, f32[64,64,128]{2,1,0:T(8,128)}, u32[]{:S(2)}) copy-start(f32[64,64,128]{2,1,0:T(8,128)} %copy-done) | copy-start | bytes 6291460
  424.2 5.3 collective-permute-start.4
  425.5 5.0 collective-permute-start.5
  430.6 6.8 collective-permute-start.6
  434.2 3.9 collective-permute-start.7
  443.6 74.2 %copy-start.16 = (f32[64,64,128]{2,1,0:T(8,128)S(1)}, f32[64,64,128]{2,1,0:T(8,128)}, u32[]{:S(2)}) copy-start(f32[64,64,128]{2,1,0:T(8,128)} %copy-done.15) | copy-start | bytes 6291460
  639.5 72.0 %copy-start.5 = (f32[64,64,128]{2,1,0:T(8,128)S(1)}, f32[64,64,128]{2,1,0:T(8,128)}, u32[]{:S(2)}) copy-start(f32[64,64,128]{2,1,0:T(8,128)} %copy-done.3) | copy-start | bytes 6291460
  714.1 17.9 %copy-start.6 = (f32[64,64,128]{2,1,0:T(8,128)}, f32[64,64,128]{2,1,0:T(8,128)S(1)}, u32[]{:S(2)}) copy-start(f32[64,64,128]{2,1,0:T(8,128)S(1)} %bitcast_add_fusion.1) | copy-start | bytes 6291460
  714.2 5.3 collective-permute-start.8
  715.5 5.0 collective-permute-start.9
  720.5 7.0 collective-permute-start.10
  724.2 4.1 collective-permute-start.11
  732.0 74.1 %copy-start.18 = (f32[64,64,128]{2,1,0:T(8,128)S(1)}, f32[64,64,128]{2,1,0:T(8,128)}, u32[]{:S(2)}) copy-start(f32[64,64,128]{2,1,0:T(8,128)} %copy-done.17) | copy-start | bytes 6291460
  927.8 71.9 %copy-start.7 = (f32[64,64,128]{2,1,0:T(8,128)S(1)}, f32[64,64,128]{2,1,0:T(8,128)}, u32[]{:S(2)}) copy-start(f32[64,64,128]{2,1,0:T(8,128)} %copy-done.6) | copy-start | bytes 6291460
  1002.3 5.3 collective-permute-start.12
  1003.6 5.0 collective-permute-start.13
  1008.7 6.8 collective-permute-start.14
  1012.4 3.8 collective-permute-start.15
  1019.9 74.2 %copy-start.2 = (f32[64,64,128]{2,1,0:T(8,128)S(1)}, f32[64,64,128]{2,1,0:T(8,128)}, u32[]{:S(2)}) copy-start(f32[64,64,128]{2,1,0:T(8,128)} %copy-done) | copy-start | bytes 6291460
  (27 other events, 123.1 us)
where the time goes:
time: 1110 us; the launch traced here: 1100 us
  blocking collectives  836 us (75%)
  other arithmetic  84.9 us (8%)
  matrix products  81.6 us (7%)
  starting transfers between devices  47.9 us (4%)
  local copies, waits for them, and re-layouts  23.2 us (2%)
    unnamed x4, blocking collectives  379 us
    psum x4, blocking collectives, inner_sum(): return lax.psum(jnp.sum(first * second), ('gx', 'gy'))  255 us
    psum x3, blocking collectives, shards(): alpha = gamma / lax.psum(jnp.sum(direction * image), ('gx', 'gy'))  201 us
    dot_general x8, matrix products, transform(): return jnp.einsum('bj,ajz->abz', table_y, step_one, precision=HIGH)  49.1 us
    dot_general x8, matrix products, transform(): step_one = jnp.einsum('ai,ijz->ajz', table_x, field, precision=HIGH)  32.5 us
    ppermute x8, starting transfers between devices, with_halo(): before = lax.ppermute(last, axis, up)  28.1 us
    reduce_sum x4, other arithmetic, shards(): alpha = gamma / lax.psum(jnp.sum(direction * image), ('gx', 'gy'))  23.2 us
  transfers between devices with their start and end apart: 16, of which 8 were waited for; matrix products, arithmetic and copies ran while one was open for 0% of the time, Pallas kernels for 0%

commit v1 on v0

v1 whole, which is shorter than its diff:
```python
import functools

import jax
import jax.numpy as jnp
import ml_dtypes
import numpy as np
from jax import lax
from jax.experimental import pallas as pl
from jax.experimental.pallas import tpu as pltpu
from jax.sharding import PartitionSpec as P

ITERS = 4
MOST = 12
LANES = 128
ROWS = 8
GATHERS = ITERS + 1
LINES = 4
PLANES = 8
F32 = jnp.float32
MESH = pl.DeviceIdType.MESH


def sine_table(count):
    index = np.arange(count, dtype=np.float64)
    angle = np.pi * (index[:, None] + 1.0) * (index[None, :] + 1.0) / (count + 1.0)
    return np.sqrt(2.0 / (count + 1.0)) * np.sin(angle)


def eigen_values(count):
    index = np.arange(count, dtype=np.float64)
    return 2.0 - 2.0 * np.cos(np.pi * (index + 1.0) / (count + 1.0))


def split_table(count):
    table = sine_table(count).astype(np.float32)
    high = table.astype(ml_dtypes.bfloat16)
    low = (table - high.astype(np.float32)).astype(ml_dtypes.bfloat16)
    return np.concatenate([np.concatenate([high, high], axis=1), np.concatenate([low, low], axis=1)], axis=0)


def transform(table, field):
    high = field.astype(jnp.bfloat16)
    low = (field - high.astype(F32)).astype(jnp.bfloat16)
    stacked = jnp.concatenate([high, low], axis=0)
    both = jnp.dot(table, stacked, preferred_element_type=F32)
    return both[:field.shape[0]] + both[field.shape[0]:]


def fold(value):
    return jnp.sum(value.reshape(-1, ROWS, LANES), axis=0)


def kernel(
    n_gx, n_gy, size,
    rhs_hbm, diag_hbm, count_hbm, flag_hbm, coarse_hbm, table_hbm, mu_hbm,
    x_ref, r_ref,
    count_ref, flag_ref, coarse_ref, table_ref, mu_ref,
    diag_ref, p_ref, s_ref, image_ref, back_ref, hat_ref, line_ref, step_ref, mode_ref, twice_ref,
    root_ref, near_ref, far_ref, mid_ref,
    edge_ref, ghost_x, ghost_y, fix_ref, small_ref, all_ref, coarse_pad,
    in_sem, halo_send, halo_recv, row_send, row_recv, col_send, col_recv,
):
    gx = lax.axis_index("gx")
    gy = lax.axis_index("gy")
    mine = gx * n_gy + gy
    pitch = size + ROWS
    odd_pitch = size + 1
    row8 = lax.broadcasted_iota(jnp.int32, (ROWS, LANES), 0)
    lane8 = lax.broadcasted_iota(jnp.int32, (ROWS, LANES), 1)

    def plane(index):
        return pl.ds(pl.multiple_of(index * size, ROWS), size)

    def padded(index):
        return pl.ds(pl.multiple_of((index + 1) * pitch, ROWS), size)

    pairs = (
        (flag_hbm, flag_ref), (mu_hbm, mu_ref), (coarse_hbm, coarse_ref), (count_hbm, count_ref),
        (table_hbm, table_ref), (rhs_hbm, r_ref), (diag_hbm, diag_ref),
    )
    loads = [pltpu.make_async_copy(source, target, in_sem.at[n]) for n, (source, target) in enumerate(pairs)]
    for load in loads:
        load.start()
    if n_gx * ROWS < LANES:
        all_ref[...] = jnp.zeros_like(all_ref)

    barrier = pltpu.get_barrier_semaphore()

    def greet_row(step, carry):
        pl.semaphore_signal(barrier, inc=1, device_id=(gx, lax.rem(gy + step, n_gy)), device_id_type=MESH)
        return carry

    def greet_col(step, carry):
        pl.semaphore_signal(barrier, inc=1, device_id=(lax.rem(gx + step, n_gx), gy), device_id_type=MESH)
        return carry

    lax.fori_loop(1, n_gy, greet_row, 0)
    lax.fori_loop(1, n_gx, greet_col, 0)

    loads[0].wait()
    loads[1].wait()
    shift = 2.5 * flag_ref[pl.ds(mine, 1), :].astype(F32) + 2.5
    lane = lax.broadcasted_iota(jnp.int32, (size, LANES), 1)

    def coefficients(b):
        d = mu_ref[...] + mu_ref[pl.ds(b, 1), :] + shift
        root = lax.rsqrt(d)
        root = root * (1.5 - 0.5 * d * root * root)
        near = jnp.where(lane == 0, 0.0, root * pltpu.roll(root, 1, 1))
        square = near * near
        root_ref[plane(b), :] = root
        near_ref[plane(b), :] = near
        far_ref[plane(b), :] = near * pltpu.roll(near, 1, 1)
        mid_ref[plane(b), :] = square + pltpu.roll(square, LANES - 1, 1)

    def coefficient_pair(t, carry):
        coefficients(2 * t)
        coefficients(2 * t + 1)
        return carry

    lax.fori_loop(0, size // 2, coefficient_pair, 0)

    back_ref[pl.ds(0, pitch), :] = jnp.zeros((pitch, LANES), F32)
    back_ref[pl.ds((size + 1) * pitch, pitch), :] = jnp.zeros((pitch, LANES), F32)

    def clear(index, carry):
        start = pl.multiple_of((index + 1) * pitch + size, ROWS)
        back_ref[pl.ds(start, ROWS), :] = jnp.zeros((ROWS, LANES), F32)
        return carry

    lax.fori_loop(0, size, clear, 0)
    coarse_pad[pl.ds(0, ROWS), :] = jnp.zeros((ROWS, LANES), F32)
    coarse_pad[pl.ds(ROWS + LANES, ROWS), :] = jnp.zeros((ROWS, LANES), F32)

    pl.semaphore_wait(barrier, n_gx + n_gy - 2)

    def row_copy(slot, step):
        return pltpu.make_async_remote_copy(
            src_ref=small_ref.at[slot, gy], dst_ref=small_ref.at[slot, gy],
            send_sem=row_send.at[slot, step], recv_sem=row_recv.at[slot, step],
            device_id=(gx, lax.rem(gy + step, n_gy)), device_id_type=MESH,
        )

    def col_copy(slot, step):
        return pltpu.make_async_remote_copy(
            src_ref=all_ref.at[slot, gx], dst_ref=all_ref.at[slot, gx],
            send_sem=col_send.at[slot, step], recv_sem=col_recv.at[slot, step],
            device_id=(lax.rem(gx + step, n_gx), gy), device_id_type=MESH,
        )

    def over(first, last, act):
        def body(step, carry):
            act(step)
            return carry

        lax.fori_loop(first, last, body, 0)

    def gather_start(slot, payload):
        small_ref[slot, gy] = jnp.where(row8 == gy, payload, 0.0)
        over(1, n_gy, lambda step: row_copy(slot, step).start())

    def gather_middle(slot):
        over(1, n_gy, lambda step: row_copy(slot, step).wait())
        total = small_ref[slot, 0]
        for other in range(1, n_gy):
            total = total + small_ref[slot, other]
        all_ref[slot, gx] = total
        over(1, n_gx, lambda step: col_copy(slot, step).start())

    def gather_end(slot):
        over(1, n_gx, lambda step: col_copy(slot, step).wait())
        return all_ref[slot].reshape(LANES, LANES)

    for load in loads[2:5]:
        load.wait()
    gather_start(ITERS, coarse_ref[...])

    count = jnp.full((ROWS, LANES), count_ref[mine], jnp.int32)

    count = jnp.concatenate([count] * (size // ROWS), axis=0)
    odd = count % 2 == 1
    active = [count > 2 * step for step in range(MOST // 2)]

    def rows(base, index):
        return pl.ds(base + index * size, size)

    def transform_all(parts):
        table = table_ref[...]
        done = []
        for n in range(0, len(parts), 2):
            both = transform(table, jnp.concatenate(parts[n:n + 2], axis=1))
            done += [both[:, :LANES], both[:, LANES:]]
        return done

    def forward(first, parts):
        for n, part in enumerate(transform_all(parts)):
            step_ref[pl.ds((first + n) * odd_pitch, size), :] = part

    def group(t):
        return pl.multiple_of(t * (LINES * size), ROWS)

    def lines_in(t, base, shift):
        first = (t + shift) * LINES
        parts = [step_ref[pl.ds(first + m, size, stride=odd_pitch), :] for m in range(LINES)]
        for m, part in enumerate(transform_all(parts)):
            hat_ref[rows(base, m + shift * LINES), :] = part

    def lines_sweep(base, shift):
        here = [rows(base, m + shift * LINES) for m in range(LINES)]
        guess = []
        for m in range(LINES):
            near = near_ref[here[m], :]
            start = hat_ref[here[m], :] * root_ref[here[m], :]
            twice = start + near * pltpu.roll(start, 1, 1) + pltpu.roll(near * start, LANES - 1, 1)
            twice_ref[pl.ds(m * size, size), :] = twice
            guess.append(jnp.where(odd, start, twice))
        for step in range(1, MOST // 2):
            for m in range(LINES):
                far = far_ref[here[m], :]
                fresh = (twice_ref[pl.ds(m * size, size), :] + mid_ref[here[m], :] * guess[m]) + (
                    far * pltpu.roll(guess[m], 2, 1) + pltpu.roll(far * guess[m], LANES - 2, 1)
                )
                guess[m] = jnp.where(active[step], fresh, guess[m])
        for m in range(LINES):
            line_ref[here[m], :] = guess[m] * root_ref[here[m], :]

    def lines_out(base, shift, first):
        parts = [line_ref[rows(base, m + shift * LINES), :] for m in range(LINES)]
        for m, part in enumerate(transform_all(parts)):
            mode_ref[pl.ds((first + m) * odd_pitch, size), :] = part

    def solve_lines():
        groups = size // LINES

        def body(t, carry):
            base = group(t)
            lines_out(base, -2, (t - 2) * LINES)
            lines_sweep(base, -1)
            lines_in(t, base, 0)
            return carry

        lines_in(0, 0, 0)
        lines_sweep(0, 0)
        lines_in(1, group(1), 0)
        lax.fori_loop(2, groups, body, 0)
        last = group(groups)
        lines_out(last, -2, size - 2 * LINES)
        lines_sweep(last, -1)
        lines_out(last, -1, size - LINES)

    def backward(first):
        parts = [mode_ref[pl.ds(first + m, size, stride=odd_pitch), :] for m in range(PLANES)]
        base = pl.multiple_of((first + 1) * pitch, ROWS)
        for m, part in enumerate(transform_all(parts)):
            back_ref[pl.ds(base + m * pitch, size), :] = part
            edge_ref[0, pl.ds(first + m, 1), :] = part[:1]
            edge_ref[1, pl.ds(first + m, 1), :] = part[size - 1:]

    def halo_copy(turn, side):
        if side < 2:
            step = 1 if side == 0 else n_gx - 1
            index = size - 1 if side == 0 else 0
            source = back_ref.at[pl.ds((index + 1) * pitch, size)]
            target = ghost_x.at[turn, side]
            device = (lax.rem(gx + step, n_gx), gy)
        else:
            step = 1 if side == 2 else n_gy - 1
            source = edge_ref.at[1 if side == 2 else 0]
            target = ghost_y.at[turn, side - 2]
            device = (gx, lax.rem(gy + step, n_gy))
        return pltpu.make_async_remote_copy(
            src_ref=source, dst_ref=target,
            send_sem=halo_send.at[turn, side], recv_sem=halo_recv.at[turn, side],
            device_id=device, device_id_type=MESH,
        )

    inside = [gx > 0, gx < n_gx - 1, gy > 0, gy < n_gy - 1]

    def ghosts(turn):
        raw = [ghost_x[turn, 0], ghost_x[turn, 1], ghost_y[turn, 0], ghost_y[turn, 1]]
        return [jnp.where(inside[n], raw[n], 0.0) for n in range(4)]

    def apply(turn, i, sums):
        here = back_ref[padded(i), :]
        start = (i + 1) * pitch
        beside = back_ref[padded(i - 1), :] + back_ref[padded(i + 1), :]
        beside = beside + back_ref[pl.ds(start - 1, size), :] + back_ref[pl.ds(start + 1, size), :]
        below = jnp.where(lane == 0, 0.0, pltpu.roll(here, 1, 1))
        above = jnp.where(lane == LANES - 1, 0.0, pltpu.roll(here, LANES - 1, 1))
        diag = diag_ref[plane(i), :]
        image = (6.0 + diag) * here - (beside + (below + above))
        image_ref[plane(i), :] = image
        resid = r_ref[plane(i), :]
        terms = [resid, resid * here, here * image, image]
        if turn:
            old = s_ref[plane(i), :]
            terms += [here * old, old]
        else:
            terms += [diag]
        return tuple(total + fold(term) for total, term in zip(sums, terms))

    big_row = lax.broadcasted_iota(jnp.int32, (LANES, LANES), 0)
    big_lane = lax.broadcasted_iota(jnp.int32, (LANES, LANES), 1)

    loads[5].wait()
    loads[6].wait()

    def first_forward(t, carry):
        base = pl.multiple_of(t * (PLANES * size), ROWS)
        forward(t * PLANES, [r_ref[rows(base, m), :] for m in range(PLANES)])
        return carry

    lax.fori_loop(0, size // PLANES, first_forward, 0)
    gather_middle(ITERS)

    diag_total = None
    gamma = None
    energy = None
    for turn in range(ITERS):
        solve_lines()

        def ends(t, carry):
            backward(t * (size - PLANES))
            return carry

        def others(t, carry):
            backward(PLANES * t)
            return carry

        lax.fori_loop(0, 2, ends, 0)
        halos = [halo_copy(turn, side) for side in range(4)]
        halos[0].start()
        halos[1].start()
        lax.fori_loop(1, size // PLANES - 1, others, 0)
        halos[2].start()
        halos[3].start()

        zeros = tuple(jnp.zeros((ROWS, LANES), F32) for _ in range(6 if turn else 5))

        def apply_some(t, sums):
            for m in range(4):
                sums = apply(turn, 4 * t + m, sums)
            return sums

        sums = list(lax.fori_loop(0, size // 4, apply_some, zeros))
        for halo in halos:
            halo.wait()
        ghost = ghosts(turn)
        faces = [back_ref[padded(0), :], back_ref[padded(size - 1), :], edge_ref[0], edge_ref[1]]
        for n in range(4):
            sums[2] = sums[2] - fold(faces[n] * ghost[n])
            sums[3] = sums[3] - fold(ghost[n])
        if turn == 0:
            diag_total = sums[4]
            sums = sums[:4] + [jnp.zeros((ROWS, LANES), F32)] * 2
        sums.append(diag_total)
        stacked = jnp.zeros((ROWS, LANES), F32)
        for n, total in enumerate(sums):
            stacked = jnp.where(row8 == n, jnp.sum(total, axis=0, keepdims=True), stacked)
        stacked = jnp.sum(stacked, axis=1, keepdims=True)
        payload = jnp.sum(jnp.where(row8 == lane8, stacked, 0.0), axis=0, keepdims=True)
        gather_start(turn, payload)
        gather_middle(turn)
        if turn == 0:
            gather_end(ITERS)
        every = gather_end(turn)

        matrix = all_ref[ITERS].reshape(LANES, LANES)
        coarse = jnp.dot(matrix, every, precision=lax.Precision.HIGHEST, preferred_element_type=F32)
        coarse = jnp.broadcast_to(coarse[:, :1], (LANES, LANES))
        coarse_pad[pl.ds(ROWS, LANES), :] = coarse
        beside = coarse_pad[pl.ds(0, LANES), :] + coarse_pad[pl.ds(2 * ROWS, LANES), :]
        beside = beside + jnp.where(big_row % ROWS == 0, 0.0, coarse_pad[pl.ds(ROWS - 1, LANES), :])
        beside = beside + jnp.where(big_row % ROWS == n_gy - 1, 0.0, coarse_pad[pl.ds(ROWS + 1, LANES), :])
        ends_total = 2.0 * size * size
        weight = jnp.where((big_lane == 0) | (big_lane == 5), coarse, 1.0)
        weight = jnp.where(big_lane == 3, 2.0 * coarse, weight)
        weight = jnp.where(big_lane == 6, coarse * coarse, weight)
        terms = every * weight
        flux = coarse * (ends_total * coarse + size * LANES * (4.0 * coarse - beside))
        terms = terms + jnp.where(big_lane == 6, flux, 0.0)
        terms = jnp.sum(terms, axis=0, keepdims=True)
        slim = lax.broadcasted_iota(jnp.int32, (1, LANES), 1)

        def pick(*lanes):
            mask = slim == lanes[0]
            for which in lanes[1:]:
                mask = mask | (slim == which)
            total = jnp.sum(jnp.where(mask, terms, 0.0), axis=1, keepdims=True)
            return jnp.broadcast_to(total, (ROWS, LANES))

        fresh = pick(0, 1)
        curve = pick(2, 3, 6)
        if turn:
            beta = fresh / gamma
            energy = curve + beta * (2.0 * pick(4, 5) + beta * energy)
        else:
            beta = None
            energy = curve
        gamma = fresh
        alpha = gamma / energy

        own = coarse_pad[pl.ds(ROWS + mine, 1), :]
        across = [
            coarse_pad[pl.ds(mine, 1), :],
            coarse_pad[pl.ds(2 * ROWS + mine, 1), :],
            jnp.where(inside[2], coarse_pad[pl.ds(ROWS - 1 + mine, 1), :], 0.0),
            jnp.where(inside[3], coarse_pad[pl.ds(ROWS + 1 + mine, 1), :], 0.0),
        ]
        fixes = [(own - across[n]) - ghost[n] for n in range(4)]
        image_ref[plane(0), :] = image_ref[plane(0), :] + fixes[0]
        image_ref[plane(size - 1), :] = image_ref[plane(size - 1), :] + fixes[1]
        fix_ref[0] = fixes[2]
        fix_ref[1] = fixes[3]

        def span(value):
            return jnp.broadcast_to(value[:1], (size, LANES))

        own_wide = jnp.broadcast_to(own, (size, LANES))
        ends_wide = jnp.where((lane == 0) | (lane == LANES - 1), 1.0, 0.0)
        alpha_wide = span(alpha)
        beta_wide = span(beta) if turn else None

        def update(base, first, m):
            here = rows(base, m)
            low = jnp.where(row8 == 0, fix_ref[0, pl.ds(first + m, 1), :], 0.0)
            high = jnp.where(row8 == ROWS - 1, fix_ref[1, pl.ds(first + m, 1), :], 0.0)
            image = image_ref[here, :]
            image = jnp.concatenate(
                [image[:ROWS] + low, image[ROWS:size - ROWS], image[size - ROWS:] + high], axis=0
            )
            image = image + own_wide * (diag_ref[here, :] + ends_wide)
            direction = back_ref[padded(first + m), :] + own_wide
            if turn:
                image = image + beta_wide * s_ref[here, :]
                direction = direction + beta_wide * p_ref[here, :]
                field = x_ref[here, :] + alpha_wide * direction
            else:
                field = alpha_wide * direction
            resid = r_ref[here, :] - alpha_wide * image
            if turn < ITERS - 1:
                s_ref[here, :] = image
                p_ref[here, :] = direction
            x_ref[here, :] = field
            r_ref[here, :] = resid
            return resid

        def update_some(t, carry):
            base = pl.multiple_of(t * (PLANES * size), ROWS)
            parts = [update(base, t * PLANES, m) for m in range(PLANES)]
            if turn < ITERS - 1:
                forward(t * PLANES, parts)
            return carry

        lax.fori_loop(0, size // PLANES, update_some, 0)


def shards(n_gx, n_gy, right_side, diagonal, sweep_counts, refine_flags, coarse_inverse):
    size, _, cells = right_side.shape
    flat = (size * size, cells)
    table = jnp.asarray(split_table(size))
    mu = jnp.asarray(np.repeat(eigen_values(size).astype(np.float32)[:, None], cells, axis=1))
    subs = n_gx * n_gy
    if coarse_inverse.shape[1] < LANES:
        coarse_inverse = jnp.pad(coarse_inverse, ((0, 0), (0, LANES - subs)))
    operands = (
        right_side.reshape(flat), diagonal.reshape(flat), sweep_counts, refine_flags, coarse_inverse, table, mu
    )
    vmem = pl.BlockSpec(memory_space=pltpu.VMEM)
    hbm = pl.BlockSpec(memory_space=pltpu.HBM)
    field = pltpu.VMEM(flat, F32)
    face = (size, LANES)
    outs = pl.pallas_call(
        functools.partial(kernel, n_gx, n_gy, size),
        out_shape=[jax.ShapeDtypeStruct(flat, F32)] * 2,
        in_specs=[hbm] * 7,
        out_specs=[vmem, vmem],
        scratch_shapes=[
            pltpu.SMEM(sweep_counts.shape, jnp.int32),
            pltpu.VMEM(refine_flags.shape, jnp.int32),
            pltpu.VMEM(coarse_inverse.shape, F32),
            pltpu.VMEM(table.shape, table.dtype),
            pltpu.VMEM(mu.shape, F32),
            field, field, field, field,
            pltpu.VMEM(((size + 2) * (size + ROWS), LANES), F32),
            field, field,
            pltpu.VMEM((size * (size + 1), LANES), F32),
            pltpu.VMEM((size * (size + 1), LANES), F32),
            pltpu.VMEM((LINES * size, LANES), F32),
            field, field, field, field,
            pltpu.VMEM((2,) + face, F32),
            pltpu.VMEM((ITERS, 2) + face, F32),
            pltpu.VMEM((ITERS, 2) + face, F32),
            pltpu.VMEM((2,) + face, F32),
            pltpu.VMEM((GATHERS, n_gy, ROWS, LANES), F32),
            pltpu.VMEM((GATHERS, LANES // ROWS, ROWS, LANES), F32),
            pltpu.VMEM((LANES + 2 * ROWS, LANES), F32),
            pltpu.SemaphoreType.DMA((7,)),
            pltpu.SemaphoreType.DMA((ITERS, 4)),
            pltpu.SemaphoreType.DMA((ITERS, 4)),
            pltpu.SemaphoreType.DMA((GATHERS, n_gy)),
            pltpu.SemaphoreType.DMA((GATHERS, n_gy)),
            pltpu.SemaphoreType.DMA((GATHERS, n_gx)),
            pltpu.SemaphoreType.DMA((GATHERS, n_gx)),
        ],
        compiler_params=pltpu.CompilerParams(
            collective_id=0, has_side_effects=True, vmem_limit_bytes=48 * 1024 * 1024
        ),
        cost_estimate=pl.CostEstimate(flops=4 * 10**9, bytes_accessed=8 * 2**20, transcendentals=0),
        name="pressure_solve",
    )(
        *(pltpu.with_memory_space_constraint(operand, pltpu.HBM) for operand in operands)
    )
    return tuple(out.reshape(right_side.shape) for out in outs)


def solution(mesh):
    return jax.shard_map(
        functools.partial(shards, mesh.shape["gx"], mesh.shape["gy"]),
        mesh=mesh,
        in_specs=(P("gx", "gy", None), P("gx", "gy", None), P(), P(), P(("gx", "gy"), None)),
        out_specs=(P("gx", "gy", None), P("gx", "gy", None)),
        check_vma=False,
    )
```

time: 1110 us -> 124 us (0.11)
  blocking collectives: 836 us -> 0 us
  Pallas kernels: 0 us -> 120 us
  other arithmetic: 84.9 us -> 0 us
  matrix products: 81.6 us -> 0 us
  starting transfers between devices: 47.9 us -> 0 us
  local copies, waits for them, and re-layouts: 23.2 us -> 2.64 us
    psum x7 -> x0, blocking collectives: 456 us -> none  [the longest x4 255 us: inner_sum(): return lax.psum(jnp.sum(first * second), ('gx', 'gy'))]
    unnamed x4 -> x0, blocking collectives: 379 us -> none
    pallas_call x0 -> x1, Pallas kernels: none -> 120 us  [shards(): pl.pallas_call(functools.partial(kernel, n_gx, n_gy, size), out_shape=[ja...]
    dot_general x16 -> x0, matrix products: 81.6 us -> none  [the longest x8 49.1 us: transform(): return jnp.einsum('bj,ajz->abz', table_y, step_one, precision=HIGH)]
    ppermute x16 -> x0, starting transfers between devices: 47.9 us -> none  [the longest x8 28.1 us: with_halo(): before = lax.ppermute(last, axis, up)]
    reduce_sum x8 -> x0, other arithmetic: 34.9 us -> none  [the longest x4 23.2 us: shards(): alpha = gamma / lax.psum(jnp.sum(direction * image), ('gx', 'gy'))]
    concatenate x8 -> x0, other arithmetic: 16.7 us -> none  [with_halo(): array = jnp.concatenate([before, array, after], axis=dim)]
    div x12 -> x0, other arithmetic: 14.9 us -> none  [sweep(): return (rhs + below + above) / scale]
  transfers between devices with their start and end apart: 16 -> 0, of which waited for: 8 -> 0; matrix products, arithmetic and copies ran while one was open for 0% -> 0% of each run, Pallas kernels for 0% -> 0%
where the time goes in v1:
time: 124 us
  Pallas kernels  120 us (97%)
  local copies, waits for them, and re-layouts  2.64 us (2%)
    pallas_call x1, Pallas kernels, shards(): pl.pallas_call(functools.partial(kernel, n_gx, n_gy, size), out_shape=[ja...  120 us
    unnamed x2, local copies, waits for them, and re-layouts  2.64 us

profile of v1, /device:TPU:1, one launch (start us, length us, event | category | flops | bytes accessed | tf_op | source)
XLA Modules:
  0.0 123.8 jit_solution(7766766567279201547)
XLA Ops:
  0.6 120.5 %pressure_solve.1 = (f32[4096,128]{1,0:T(8,128)S(1)}, f32[4096,128]{1,0:T(8,128)S(1)}) custom-call(f32[4096,128]{1,0:T(8,128)} %bitcast.6, f32[4096,128]{1,0:T(8,128)} %bitcast.7, s32[128]{0:T(128)} %count_hbm.1, s32[128,128]{1,0:T(8,128)} %flag_hbm.1, f32[1,128]{1,0:T(1,128)} %coarse_hbm.1, bf16[128,128]{1,0:T(8,128)(2,1)} %constant.4.clone.table_hbm, ...), custom_call_target="tpu_custom_call" | custom-call | flops 4000000000 | bytes 8388608 | tf_op jit(solution)/shard_map/pressure_solve/pallas_call | solution.py:473
  121.1 1.3 %copy.11 = f32[64,64,128]{2,1,0:T(8,128)} copy(f32[64,64,128]{2,1,0:T(8,128)S(1)} %bitcast.5) | data formatting | bytes 4194304
  122.4 1.3 %copy.12 = f32[64,64,128]{2,1,0:T(8,128)} copy(f32[64,64,128]{2,1,0:T(8,128)S(1)} %bitcast.4) | data formatting | bytes 4194304

commit v2 on v1

--- a/solution.py
+++ b/solution.py
@@ -15,7 +15,9 @@
 ROWS = 8
 GATHERS = ITERS + 1
 LINES = 4
-PLANES = 8
+GROUPS = 2
+PLANES = 16
+APPLIES = 8
 F32 = jnp.float32
 MESH = pl.DeviceIdType.MESH
 
@@ -132,6 +134,13 @@
     coarse_pad[pl.ds(0, ROWS), :] = jnp.zeros((ROWS, LANES), F32)
     coarse_pad[pl.ds(ROWS + LANES, ROWS), :] = jnp.zeros((ROWS, LANES), F32)
 
+    def wipe(t, carry):
+        here = pl.ds(pl.multiple_of(t * (4 * size), ROWS), 4 * size)
+        for field in (p_ref, s_ref, x_ref):
+            field[here, :] = jnp.zeros((4 * size, LANES), F32)
+        return carry
+
+    lax.fori_loop(0, size // 4, wipe, 0)
     pl.semaphore_wait(barrier, n_gx + n_gy - 2)
 
     def row_copy(slot, step):
@@ -160,7 +169,7 @@
         over(1, n_gy, lambda step: row_copy(slot, step).start())
 
     def gather_middle(slot):
-        over(1, n_gy, lambda step: row_copy(slot, step).wait())
+        over(1, n_gy, lambda step: row_copy(slot, step).wait_recv())
         total = small_ref[slot, 0]
         for other in range(1, n_gy):
             total = total + small_ref[slot, other]
@@ -168,8 +177,12 @@
         over(1, n_gx, lambda step: col_copy(slot, step).start())
 
     def gather_end(slot):
-        over(1, n_gx, lambda step: col_copy(slot, step).wait())
+        over(1, n_gx, lambda step: col_copy(slot, step).wait_recv())
         return all_ref[slot].reshape(LANES, LANES)
+
+    def gather_drain(slot):
+        over(1, n_gy, lambda step: row_copy(slot, step).wait_send())
+        over(1, n_gx, lambda step: col_copy(slot, step).wait_send())
 
     for load in loads[2:5]:
         load.wait()
@@ -196,57 +209,54 @@
         for n, part in enumerate(transform_all(parts)):
             step_ref[pl.ds((first + n) * odd_pitch, size), :] = part
 
-    def group(t):
-        return pl.multiple_of(t * (LINES * size), ROWS)
-
-    def lines_in(t, base, shift):
-        first = (t + shift) * LINES
-        parts = [step_ref[pl.ds(first + m, size, stride=odd_pitch), :] for m in range(LINES)]
+    def lines_in(first, base, shift):
+        parts = [step_ref[pl.ds(first + m, size, stride=odd_pitch), :] for m in range(GROUPS * LINES)]
         for m, part in enumerate(transform_all(parts)):
-            hat_ref[rows(base, m + shift * LINES), :] = part
+            hat_ref[rows(base, m + shift), :] = part
 
     def lines_sweep(base, shift):
-        here = [rows(base, m + shift * LINES) for m in range(LINES)]
-        guess = []
-        for m in range(LINES):
-            near = near_ref[here[m], :]
-            start = hat_ref[here[m], :] * root_ref[here[m], :]
-            twice = start + near * pltpu.roll(start, 1, 1) + pltpu.roll(near * start, LANES - 1, 1)
-            twice_ref[pl.ds(m * size, size), :] = twice
-            guess.append(jnp.where(odd, start, twice))
-        for step in range(1, MOST // 2):
+        for part in range(GROUPS):
+            here = [rows(base, m + part * LINES + shift) for m in range(LINES)]
+            kept = [pl.ds((part * LINES + m) * size, size) for m in range(LINES)]
+            guess = []
             for m in range(LINES):
-                far = far_ref[here[m], :]
-                fresh = (twice_ref[pl.ds(m * size, size), :] + mid_ref[here[m], :] * guess[m]) + (
-                    far * pltpu.roll(guess[m], 2, 1) + pltpu.roll(far * guess[m], LANES - 2, 1)
-                )
-                guess[m] = jnp.where(active[step], fresh, guess[m])
-        for m in range(LINES):
-            line_ref[here[m], :] = guess[m] * root_ref[here[m], :]
-
-    def lines_out(base, shift, first):
-        parts = [line_ref[rows(base, m + shift * LINES), :] for m in range(LINES)]
+                near = near_ref[here[m], :]
+                start = hat_ref[here[m], :] * root_ref[here[m], :]
+                twice = start + near * pltpu.roll(start, 1, 1) + pltpu.roll(near * start, LANES - 1, 1)
+                twice_ref[kept[m], :] = twice
+                guess.append(jnp.where(odd, start, twice))
+            for step in range(1, MOST // 2):
+                for m in range(LINES):
+                    far = far_ref[here[m], :]
+                    fresh = (twice_ref[kept[m], :] + mid_ref[here[m], :] * guess[m]) + (
+                        far * pltpu.roll(guess[m], 2, 1) + pltpu.roll(far * guess[m], LANES - 2, 1)
+                    )
+                    guess[m] = jnp.where(active[step], fresh, guess[m])
+            for m in range(LINES):
+                line_ref[here[m], :] = guess[m] * root_ref[here[m], :]
+
+    def lines_out(first, base, shift):
+        parts = [line_ref[rows(base, m + shift), :] for m in range(GROUPS * LINES)]
         for m, part in enumerate(transform_all(parts)):
             mode_ref[pl.ds((first + m) * odd_pitch, size), :] = part
 
     def solve_lines():
-        groups = size // LINES
+        many = GROUPS * LINES
 
         def body(t, carry):
-            base = group(t)
-            lines_out(base, -2, (t - 2) * LINES)
-            lines_sweep(base, -1)
-            lines_in(t, base, 0)
+            base = pl.multiple_of(t * (many * size), ROWS)
+            lines_out((t - 2) * many, base, -2 * many)
+            lines_sweep(base, -many)
+            lines_in(t * many, base, 0)
             return carry
 
         lines_in(0, 0, 0)
         lines_sweep(0, 0)
-        lines_in(1, group(1), 0)
-        lax.fori_loop(2, groups, body, 0)
-        last = group(groups)
-        lines_out(last, -2, size - 2 * LINES)
-        lines_sweep(last, -1)
-        lines_out(last, -1, size - LINES)
+        lines_in(many, many * size, 0)
+        lax.fori_loop(2, size // many, body, 0)
+        lines_out(size - 2 * many, size * size, -2 * many)
+        lines_sweep(size * size, -many)
+        lines_out(size - many, size * size, -many)
 
     def backward(first):
         parts = [mode_ref[pl.ds(first + m, size, stride=odd_pitch), :] for m in range(PLANES)]
@@ -280,7 +290,7 @@
         raw = [ghost_x[turn, 0], ghost_x[turn, 1], ghost_y[turn, 0], ghost_y[turn, 1]]
         return [jnp.where(inside[n], raw[n], 0.0) for n in range(4)]
 
-    def apply(turn, i, sums):
+    def apply(i, sums):
         here = back_ref[padded(i), :]
         start = (i + 1) * pitch
         beside = back_ref[padded(i - 1), :] + back_ref[padded(i + 1), :]
@@ -291,12 +301,8 @@
         image = (6.0 + diag) * here - (beside + (below + above))
         image_ref[plane(i), :] = image
         resid = r_ref[plane(i), :]
-        terms = [resid, resid * here, here * image, image]
-        if turn:
-            old = s_ref[plane(i), :]
-            terms += [here * old, old]
-        else:
-            terms += [diag]
+        old = s_ref[plane(i), :]
+        terms = [resid, resid * here, here * image, image, here * old, old]
         return tuple(total + fold(term) for total, term in zip(sums, terms))
 
     big_row = lax.broadcasted_iota(jnp.int32, (LANES, LANES), 0)
@@ -305,18 +311,20 @@
     loads[5].wait()
     loads[6].wait()
 
-    def first_forward(t, carry):
+    def first_forward(t, total):
         base = pl.multiple_of(t * (PLANES * size), ROWS)
         forward(t * PLANES, [r_ref[rows(base, m), :] for m in range(PLANES)])
-        return carry
-
-    lax.fori_loop(0, size // PLANES, first_forward, 0)
+        for m in range(PLANES):
+            total = total + fold(diag_ref[rows(base, m), :])
+        return total
+
+    diag_total = lax.fori_loop(0, size // PLANES, first_forward, jnp.zeros((ROWS, LANES), F32))
     gather_middle(ITERS)
-
-    diag_total = None
-    gamma = None
-    energy = None
-    for turn in range(ITERS):
+    slim = lax.broadcasted_iota(jnp.int32, (1, LANES), 1)
+    ends_wide = jnp.where((lane == 0) | (lane == LANES - 1), 1.0, 0.0)
+
+    def iterate(turn, scalars):
+        gamma, energy = scalars
         solve_lines()
 
         def ends(t, carry):
@@ -335,24 +343,20 @@
         halos[2].start()
         halos[3].start()
 
-        zeros = tuple(jnp.zeros((ROWS, LANES), F32) for _ in range(6 if turn else 5))
-
         def apply_some(t, sums):
-            for m in range(4):
-                sums = apply(turn, 4 * t + m, sums)
+            for m in range(APPLIES):
+                sums = apply(APPLIES * t + m, sums)
             return sums
 
-        sums = list(lax.fori_loop(0, size // 4, apply_some, zeros))
+        zeros = tuple(jnp.zeros((ROWS, LANES), F32) for _ in range(6))
+        sums = list(lax.fori_loop(0, size // APPLIES, apply_some, zeros))
         for halo in halos:
-            halo.wait()
+            halo.wait_recv()
         ghost = ghosts(turn)
         faces = [back_ref[padded(0), :], back_ref[padded(size - 1), :], edge_ref[0], edge_ref[1]]
         for n in range(4):
             sums[2] = sums[2] - fold(faces[n] * ghost[n])
             sums[3] = sums[3] - fold(ghost[n])
-        if turn == 0:
-            diag_total = sums[4]
-            sums = sums[:4] + [jnp.zeros((ROWS, LANES), F32)] * 2
         sums.append(diag_total)
         stacked = jnp.zeros((ROWS, LANES), F32)
         for n, total in enumerate(sums):
@@ -361,8 +365,14 @@
         payload = jnp.sum(jnp.where(row8 == lane8, stacked, 0.0), axis=0, keepdims=True)
         gather_start(turn, payload)
         gather_middle(turn)
-        if turn == 0:
+
+        @pl.when(turn == 0)
+        def _():
             gather_end(ITERS)
+            gather_drain(ITERS)
+
+        for halo in halos:
+            halo.wait_send()
         every = gather_end(turn)
 
         matrix = all_ref[ITERS].reshape(LANES, LANES)
@@ -380,7 +390,6 @@
         flux = coarse * (ends_total * coarse + size * LANES * (4.0 * coarse - beside))
         terms = terms + jnp.where(big_lane == 6, flux, 0.0)
         terms = jnp.sum(terms, axis=0, keepdims=True)
-        slim = lax.broadcasted_iota(jnp.int32, (1, LANES), 1)
 
         def pick(*lanes):
             mask = slim == lanes[0]
@@ -390,15 +399,9 @@
             return jnp.broadcast_to(total, (ROWS, LANES))
 
         fresh = pick(0, 1)
-        curve = pick(2, 3, 6)
-        if turn:
-            beta = fresh / gamma
-            energy = curve + beta * (2.0 * pick(4, 5) + beta * energy)
-        else:
-            beta = None
-            energy = curve
-        gamma = fresh
-        alpha = gamma / energy
+        beta = fresh / gamma
+        energy = pick(2, 3, 6) + beta * (2.0 * pick(4, 5) + beta * energy)
+        alpha = fresh / energy
 
         own = coarse_pad[pl.ds(ROWS + mine, 1), :]
         across = [
@@ -412,47 +415,57 @@
         image_ref[plane(size - 1), :] = image_ref[plane(size - 1), :] + fixes[1]
         fix_ref[0] = fixes[2]
         fix_ref[1] = fixes[3]
-
-        def span(value):
-            return jnp.broadcast_to(value[:1], (size, LANES))
-
         own_wide = jnp.broadcast_to(own, (size, LANES))
-        ends_wide = jnp.where((lane == 0) | (lane == LANES - 1), 1.0, 0.0)
-        alpha_wide = span(alpha)
-        beta_wide = span(beta) if turn else None
-
-        def update(base, first, m):
-            here = rows(base, m)
-            low = jnp.where(row8 == 0, fix_ref[0, pl.ds(first + m, 1), :], 0.0)
-            high = jnp.where(row8 == ROWS - 1, fix_ref[1, pl.ds(first + m, 1), :], 0.0)
-            image = image_ref[here, :]
-            image = jnp.concatenate(
-                [image[:ROWS] + low, image[ROWS:size - ROWS], image[size - ROWS:] + high], axis=0
-            )
-            image = image + own_wide * (diag_ref[here, :] + ends_wide)
-            direction = back_ref[padded(first + m), :] + own_wide
-            if turn:
-                image = image + beta_wide * s_ref[here, :]
-                direction = direction + beta_wide * p_ref[here, :]
-                field = x_ref[here, :] + alpha_wide * direction
-            else:
-                field = alpha_wide * direction
-            resid = r_ref[here, :] - alpha_wide * image
-            if turn < ITERS - 1:
-                s_ref[here, :] = image
-                p_ref[here, :] = direction
-            x_ref[here, :] = field
-            r_ref[here, :] = resid
-            return resid
-
-        def update_some(t, carry):
+        alpha_wide = jnp.broadcast_to(alpha[:1], (size, LANES))
+        beta_wide = jnp.broadcast_to(beta[:1], (size, LANES))
+
+        def update(t, keep):
             base = pl.multiple_of(t * (PLANES * size), ROWS)
-            parts = [update(base, t * PLANES, m) for m in range(PLANES)]
-            if turn < ITERS - 1:
-                forward(t * PLANES, parts)
-            return carry
-
-        lax.fori_loop(0, size // PLANES, update_some, 0)
+            for m in range(PLANES):
+                here = rows(base, m)
+                index = t * PLANES + m
+                low = jnp.where(row8 == 0, fix_ref[0, pl.ds(index, 1), :], 0.0)
+                high = jnp.where(row8 == ROWS - 1, fix_ref[1, pl.ds(index, 1), :], 0.0)
+                image = image_ref[here, :]
+                image = jnp.concatenate(
+                    [image[:ROWS] + low, image[ROWS:size - ROWS], image[size - ROWS:] + high], axis=0
+                )
+                image = image + own_wide * (diag_ref[here, :] + ends_wide) + beta_wide * s_ref[here, :]
+                direction = back_ref[padded(index), :] + own_wide + beta_wide * p_ref[here, :]
+                if keep:
+                    s_ref[here, :] = image
+                    p_ref[here, :] = direction
+                x_ref[here, :] = x_ref[here, :] + alpha_wide * direction
+                r_ref[here, :] = r_ref[here, :] - alpha_wide * image
+
+        def forward_some(t, shift):
+            base = pl.multiple_of(t * (PLANES * size), ROWS)
+            forward((t + shift) * PLANES, [r_ref[rows(base, m + shift * PLANES), :] for m in range(PLANES)])
+
+        @pl.when(turn < ITERS - 1)
+        def _():
+            def body(t, carry):
+                forward_some(t, -1)
+                update(t, True)
+                return carry
+
+            update(0, True)
+            lax.fori_loop(1, size // PLANES, body, 0)
+            forward_some(size // PLANES - 1, 0)
+
+        @pl.when(turn == ITERS - 1)
+        def _():
+            def body(t, carry):
+                update(t, False)
+                return carry
+
+            lax.fori_loop(0, size // PLANES, body, 0)
+
+        gather_drain(turn)
+        return fresh, energy
+
+    one = jnp.ones((ROWS, LANES), F32)
+    lax.fori_loop(0, ITERS, iterate, (one, jnp.zeros((ROWS, LANES), F32)))
 
 
 def shards(n_gx, n_gy, right_side, diagonal, sweep_counts, refine_flags, coarse_inverse):
@@ -486,7 +499,7 @@
             field, field,
             pltpu.VMEM((size * (size + 1), LANES), F32),
             pltpu.VMEM((size * (size + 1), LANES), F32),
-            pltpu.VMEM((LINES * size, LANES), F32),
+            pltpu.VMEM((GROUPS * LINES * size, LANES), F32),
             field, field, field, field,
             pltpu.VMEM((2,) + face, F32),
             pltpu.VMEM((ITERS, 2) + face, F32),

time: 124 us -> 120 us (0.968)
  Pallas kernels: 120 us -> 116 us
    pallas_call x1, Pallas kernels: 120 us -> 116 us  [shards(): pl.pallas_call(functools.partial(kernel, n_gx, n_gy, size), out_shape=[ja...]
where the time goes in v2:
time: 120 us
  Pallas kernels  116 us (97%)
  local copies, waits for them, and re-layouts  2.64 us (2%)
    pallas_call x1, Pallas kernels, shards(): pl.pallas_call(functools.partial(kernel, n_gx, n_gy, size), out_shape=[ja...  116 us
    unnamed x2, local copies, waits for them, and re-layouts  2.64 us

profile of v2, /device:TPU:1, one launch (start us, length us, event | category | flops | bytes accessed | tf_op | source)
XLA Modules:
  0.0 119.6 jit_solution(6194790218930915044)
XLA Ops:
  0.6 116.3 %pressure_solve.1 = (f32[4096,128]{1,0:T(8,128)S(1)}, f32[4096,128]{1,0:T(8,128)S(1)}) custom-call(f32[4096,128]{1,0:T(8,128)} %bitcast.6, f32[4096,128]{1,0:T(8,128)} %bitcast.7, s32[128]{0:T(128)} %count_hbm.1, s32[128,128]{1,0:T(8,128)} %flag_hbm.1, f32[1,128]{1,0:T(1,128)} %coarse_hbm.1, bf16[128,128]{1,0:T(8,128)(2,1)} %constant.4.clone.table_hbm, ...), custom_call_target="tpu_custom_call" | custom-call | flops 4000000000 | bytes 8388608 | tf_op jit(solution)/shard_map/pressure_solve/pallas_call | solution.py:486
  116.9 1.3 %copy.11 = f32[64,64,128]{2,1,0:T(8,128)} copy(f32[64,64,128]{2,1,0:T(8,128)S(1)} %bitcast.5) | data formatting | bytes 4194304
  118.3 1.3 %copy.12 = f32[64,64,128]{2,1,0:T(8,128)} copy(f32[64,64,128]{2,1,0:T(8,128)S(1)} %bitcast.4) | data formatting | bytes 4194304

commit v3 on v2

v3 whole, which is shorter than its diff:
```python
import functools

import jax
import jax.numpy as jnp
import ml_dtypes
import numpy as np
from jax import lax
from jax.experimental import pallas as pl
from jax.experimental.pallas import tpu as pltpu
from jax.sharding import PartitionSpec as P

ITERS = 4
MOST = 12
LANES = 128
ROWS = 8
GATHERS = ITERS + 2
SUM_LANE = 3
LINES = 4
COLUMNS = 8
PLANES = 16
APPLIES = 8
UPDATES = 8
F32 = jnp.float32
MESH = pl.DeviceIdType.MESH


def sine_table(count):
    index = np.arange(count, dtype=np.float64)
    angle = np.pi * (index[:, None] + 1.0) * (index[None, :] + 1.0) / (count + 1.0)
    return np.sqrt(2.0 / (count + 1.0)) * np.sin(angle)


def eigen_values(count):
    index = np.arange(count, dtype=np.float64)
    return 2.0 - 2.0 * np.cos(np.pi * (index + 1.0) / (count + 1.0))


def split_table(count):
    table = sine_table(count).astype(np.float32)
    high = table.astype(ml_dtypes.bfloat16)
    low = (table - high.astype(np.float32)).astype(ml_dtypes.bfloat16)
    return np.concatenate([np.concatenate([high, high], axis=1), np.concatenate([low, low], axis=1)], axis=0)


def transform(table, field):
    high = field.astype(jnp.bfloat16)
    low = (field - high.astype(F32)).astype(jnp.bfloat16)
    stacked = jnp.concatenate([high, low], axis=0)
    both = jnp.dot(table, stacked, preferred_element_type=F32)
    return both[:field.shape[0]] + both[field.shape[0]:]


def fold(value):
    return jnp.sum(value.reshape(-1, ROWS, LANES), axis=0)


def kernel(
    n_gx, n_gy, size,
    rhs_hbm, diag_hbm, count_hbm, flag_hbm, coarse_hbm, table_hbm, mu_hbm,
    x_ref, r_ref,
    count_ref, flag_ref, coarse_ref, table_ref, mu_ref,
    diag_ref, p_ref, s_ref, image_ref, back_ref, hat_ref, hat_s_ref, hat_r_ref, line_ref, step_ref, mode_ref,
    twice_ref, root_ref, near_ref, far_ref, mid_ref,
    edge_ref, ghost_x, ghost_y, small_ref, all_ref, known_ref,
    in_sem, halo_send, halo_recv, row_send, row_recv, col_send, col_recv,
):
    gx = lax.axis_index("gx")
    gy = lax.axis_index("gy")
    mine = gx * n_gy + gy
    pitch = size + ROWS
    odd_pitch = size + 1
    plain = size * size
    roomy = (size + 2) * pitch
    row8 = lax.broadcasted_iota(jnp.int32, (ROWS, LANES), 0)
    lane8 = lax.broadcasted_iota(jnp.int32, (ROWS, LANES), 1)
    lane = lax.broadcasted_iota(jnp.int32, (size, LANES), 1)
    slim = lax.broadcasted_iota(jnp.int32, (1, LANES), 1)

    def plane(index):
        return pl.ds(pl.multiple_of(index * size, ROWS), size)

    def rows(base, index):
        return pl.ds(base + index * size, size)

    def image_base(parity, first):
        return pl.multiple_of(parity * plain + first * size, ROWS)

    def back_base(parity, first):
        return pl.multiple_of(parity * roomy + (first + 1) * pitch, ROWS)

    pairs = (
        (rhs_hbm, r_ref), (flag_hbm, flag_ref), (mu_hbm, mu_ref), (coarse_hbm, coarse_ref), (count_hbm, count_ref),
        (table_hbm, table_ref), (diag_hbm, diag_ref),
    )
    loads = [pltpu.make_async_copy(source, target, in_sem.at[n]) for n, (source, target) in enumerate(pairs)]
    for load in loads:
        load.start()
    if n_gx * ROWS < LANES:
        all_ref[...] = jnp.zeros_like(all_ref)

    barrier = pltpu.get_barrier_semaphore()

    def over(first, last, act):
        def body(step, carry):
            act(step)
            return carry

        lax.fori_loop(first, last, body, 0)

    def beside_row(step):
        return gx, lax.rem(gy + step, n_gy)

    def beside_col(step):
        return lax.rem(gx + step, n_gx), gy

    def greet(device):
        pl.semaphore_signal(barrier, inc=1, device_id=device, device_id_type=MESH)

    over(1, n_gy, lambda step: greet(beside_row(step)))
    over(1, n_gx, lambda step: greet(beside_col(step)))

    def row_copy(slot, step):
        return pltpu.make_async_remote_copy(
            src_ref=small_ref.at[slot, gy], dst_ref=small_ref.at[slot, gy],
            send_sem=row_send.at[slot, step], recv_sem=row_recv.at[slot, step],
            device_id=beside_row(step), device_id_type=MESH,
        )

    def col_copy(slot, step):
        return pltpu.make_async_remote_copy(
            src_ref=all_ref.at[slot, gx], dst_ref=all_ref.at[slot, gx],
            send_sem=col_send.at[slot, step], recv_sem=col_recv.at[slot, step],
            device_id=beside_col(step), device_id_type=MESH,
        )

    def gather_start(slot, payload):
        small_ref[slot, gy] = jnp.where(row8 == gy, payload, 0.0)
        over(1, n_gy, lambda step: row_copy(slot, step).start())

    def gather_middle(slot):
        over(1, n_gy, lambda step: row_copy(slot, step).wait_recv())
        total = small_ref[slot, 0]
        for other in range(1, n_gy):
            total = total + small_ref[slot, other]
        all_ref[slot, gx] = total
        over(1, n_gx, lambda step: col_copy(slot, step).start())

    def gather_end(slot):
        over(1, n_gx, lambda step: col_copy(slot, step).wait_recv())
        return all_ref[slot].reshape(LANES, LANES)

    def gather_drain(slot):
        over(1, n_gy, lambda step: row_copy(slot, step).wait_send())
        over(1, n_gx, lambda step: col_copy(slot, step).wait_send())

    def lane_pick(row, which):
        total = jnp.sum(jnp.where(slim == which, row, 0.0), axis=1, keepdims=True)
        return jnp.broadcast_to(total, (ROWS, LANES))

    loads[0].wait()

    def add_up(t, total):
        base = pl.multiple_of(t * (8 * size), ROWS)
        for m in range(8):
            total = total + fold(r_ref[rows(base, m), :])
        return total

    total = lax.fori_loop(0, size // 8, add_up, jnp.zeros((ROWS, LANES), F32))
    total = jnp.sum(jnp.sum(total, axis=0, keepdims=True), axis=1, keepdims=True)
    for load in loads[1:6]:
        load.wait()
    pl.semaphore_wait(barrier, n_gx + n_gy - 2)
    gather_start(ITERS, coarse_ref[...])
    gather_start(ITERS + 1, jnp.where(slim == SUM_LANE, total, 0.0))

    shift = 2.5 * flag_ref[pl.ds(mine, 1), :].astype(F32) + 2.5

    def coefficients(b):
        d = mu_ref[...] + mu_ref[pl.ds(b, 1), :] + shift
        root = lax.rsqrt(d)
        root = root * (1.5 - 0.5 * d * root * root)
        near = jnp.where(lane == 0, 0.0, root * pltpu.roll(root, 1, 1))
        square = near * near
        root_ref[plane(b), :] = root
        near_ref[plane(b), :] = near
        far_ref[plane(b), :] = near * pltpu.roll(near, 1, 1)
        mid_ref[plane(b), :] = square + pltpu.roll(square, LANES - 1, 1)

    def coefficient_some(t, carry):
        for m in range(4):
            coefficients(4 * t + m)
        return carry

    lax.fori_loop(0, size // 4, coefficient_some, 0)

    def wipe(t, carry):
        here = pl.ds(pl.multiple_of(t * (4 * size), ROWS), 4 * size)
        for field in (p_ref, s_ref, x_ref, hat_s_ref, hat_r_ref):
            field[here, :] = jnp.zeros((4 * size, LANES), F32)
        return carry

    lax.fori_loop(0, size // 4, wipe, 0)

    for parity in range(2):
        back_ref[pl.ds(parity * roomy, pitch), :] = jnp.zeros((pitch, LANES), F32)
        back_ref[pl.ds(parity * roomy + (size + 1) * pitch, pitch), :] = jnp.zeros((pitch, LANES), F32)

    def clear(index, carry):
        for parity in range(2):
            start = pl.multiple_of(parity * roomy + (index + 1) * pitch + size, ROWS)
            back_ref[pl.ds(start, ROWS), :] = jnp.zeros((ROWS, LANES), F32)
        return carry

    lax.fori_loop(0, size, clear, 0)
    gather_middle(ITERS)
    gather_middle(ITERS + 1)

    count = jnp.full((ROWS, LANES), count_ref[mine], jnp.int32)
    count = jnp.concatenate([count] * (size // ROWS), axis=0)
    odd = count % 2 == 1
    active = [count > 2 * step for step in range(MOST // 2)]

    def transform_all(parts):
        table = table_ref[...]
        done = []
        for n in range(0, len(parts), 2):
            both = transform(table, jnp.concatenate(parts[n:n + 2], axis=1))
            done += [both[:, :LANES], both[:, LANES:]]
        return done

    def odd_base(first):
        return pl.multiple_of(first * odd_pitch, ROWS)

    def forward_y(source, parity):
        def body(t, carry):
            base = image_base(parity, t * PLANES)
            target = odd_base(t * PLANES)
            parts = [source[rows(base, m), :] for m in range(PLANES)]
            for m, part in enumerate(transform_all(parts)):
                step_ref[pl.ds(target + m * odd_pitch, size), :] = part
            return carry

        lax.fori_loop(0, size // PLANES, body, 0)

    def forward_x():
        def body(t, carry):
            first = t * COLUMNS
            base = pl.multiple_of(first * size, ROWS)
            parts = [step_ref[pl.ds(first + m, size, stride=odd_pitch), :] for m in range(COLUMNS)]
            for m, part in enumerate(transform_all(parts)):
                hat_ref[rows(base, m), :] = part
            return carry

        lax.fori_loop(0, size // COLUMNS, body, 0)

    def lines_sweep(base, shift, alpha, beta, sums):
        sums = list(sums)
        for part in range(0, COLUMNS, LINES):
            here = [rows(base, m + part + shift) for m in range(LINES)]
            kept = [pl.ds((part + m) * size, size) for m in range(LINES)]
            guess = []
            for m in range(LINES):
                hat_s = hat_ref[here[m], :] + beta * hat_s_ref[here[m], :]
                hat_r = hat_r_ref[here[m], :] - alpha * hat_s
                hat_s_ref[here[m], :] = hat_s
                hat_r_ref[here[m], :] = hat_r
                near = near_ref[here[m], :]
                start = hat_r * root_ref[here[m], :]
                twice = start + near * pltpu.roll(start, 1, 1) + pltpu.roll(near * start, LANES - 1, 1)
                twice_ref[kept[m], :] = twice
                guess.append(jnp.where(odd, start, twice))
            for step in range(1, MOST // 2):
                for m in range(LINES):
                    far = far_ref[here[m], :]
                    fresh = (twice_ref[kept[m], :] + mid_ref[here[m], :] * guess[m]) + (
                        far * pltpu.roll(guess[m], 2, 1) + pltpu.roll(far * guess[m], LANES - 2, 1)
                    )
                    guess[m] = jnp.where(active[step], fresh, guess[m])
            for m in range(LINES):
                line = guess[m] * root_ref[here[m], :]
                line_ref[here[m], :] = line
                sums[0] = sums[0] + fold(line * hat_r_ref[here[m], :])
                sums[1] = sums[1] + fold(line * hat_s_ref[here[m], :])
        return tuple(sums)

    def lines_out(base, shift, target):
        parts = [line_ref[rows(base, m + shift), :] for m in range(COLUMNS)]
        for m, part in enumerate(transform_all(parts)):
            mode_ref[pl.ds(target + m * odd_pitch, size), :] = part

    def solve_lines(alpha, beta):
        alpha = jnp.broadcast_to(alpha[:1], (size, LANES))
        beta = jnp.broadcast_to(beta[:1], (size, LANES))

        def body(t, sums):
            base = pl.multiple_of(t * (COLUMNS * size), ROWS)
            lines_out(base, -COLUMNS, odd_base((t - 1) * COLUMNS))
            return lines_sweep(base, 0, alpha, beta, sums)

        zeros = (jnp.zeros((ROWS, LANES), F32),) * 2
        sums = lines_sweep(0, 0, alpha, beta, zeros)
        sums = lax.fori_loop(1, size // COLUMNS, body, sums)
        lines_out(plain, -COLUMNS, (size - COLUMNS) * odd_pitch)
        return sums

    def backward(parity, first, own):
        parts = [mode_ref[pl.ds(first + m, size, stride=odd_pitch), :] for m in range(PLANES)]
        base = back_base(parity, first)
        for m, part in enumerate(transform_all(parts)):
            part = part + own
            back_ref[pl.ds(base + m * pitch, size), :] = part
            edge_ref[0, pl.ds(first + m, 1), :] = part[:1]
            edge_ref[1, pl.ds(first + m, 1), :] = part[size - 1:]

    def halo_copy(turn, side):
        if side < 2:
            device = beside_col(1 if side == 0 else n_gx - 1)
            source = back_ref.at[pl.ds(back_base(turn % 2, size - 1 if side == 0 else 0), size)]
            target = ghost_x.at[turn, side]
        else:
            device = beside_row(1 if side == 2 else n_gy - 1)
            source = edge_ref.at[1 if side == 2 else 0]
            target = ghost_y.at[turn, side - 2]
        return pltpu.make_async_remote_copy(
            src_ref=source, dst_ref=target,
            send_sem=halo_send.at[turn, side], recv_sem=halo_recv.at[turn, side],
            device_id=device, device_id_type=MESH,
        )

    inside = [gx > 0, gx < n_gx - 1, gy > 0, gy < n_gy - 1]

    def ghosts(turn):
        raw = [ghost_x[turn, 0], ghost_x[turn, 1], ghost_y[turn, 0], ghost_y[turn, 1]]
        return [jnp.where(inside[n], raw[n], 0.0) for n in range(4)]

    def apply(parity, i, sums):
        start = back_base(parity, i)
        here = back_ref[pl.ds(start, size), :]
        beside = back_ref[pl.ds(start - pitch, size), :] + back_ref[pl.ds(start + pitch, size), :]
        beside = beside + back_ref[pl.ds(start - 1, size), :] + back_ref[pl.ds(start + 1, size), :]
        below = jnp.where(lane == 0, 0.0, pltpu.roll(here, 1, 1))
        above = jnp.where(lane == LANES - 1, 0.0, pltpu.roll(here, LANES - 1, 1))
        image = (6.0 + diag_ref[plane(i), :]) * here - (beside + (below + above))
        image_ref[pl.ds(image_base(parity, i), size), :] = image
        return sums[0] + fold(here * image), sums[1] + fold(image)

    def update(parity, alpha, beta):
        alpha = jnp.broadcast_to(alpha[:1], (size, LANES))
        beta = jnp.broadcast_to(beta[:1], (size, LANES))

        def body(t, carry):
            base = pl.multiple_of(t * (UPDATES * size), ROWS)
            image = image_base(parity, t * UPDATES)
            back = back_base(parity, t * UPDATES)
            for m in range(UPDATES):
                here = rows(base, m)
                moved = image_ref[rows(image, m), :] + beta * s_ref[here, :]
                direction = back_ref[pl.ds(back + m * pitch, size), :] + beta * p_ref[here, :]
                s_ref[here, :] = moved
                p_ref[here, :] = direction
                x_ref[here, :] = x_ref[here, :] + alpha * direction
                r_ref[here, :] = r_ref[here, :] - alpha * moved
            return carry

        lax.fori_loop(0, size // UPDATES, body, 0)

    forward_y(r_ref, 0)
    forward_x()
    loads[6].wait()
    gather_end(ITERS)
    sums = gather_end(ITERS + 1)

    def spread(matrix):
        return jnp.broadcast_to(matrix[:, SUM_LANE:SUM_LANE + 1], (LANES, LANES))

    def coarse_solve():
        known_ref[2] = jnp.dot(
            all_ref[ITERS].reshape(LANES, LANES), known_ref[0],
            precision=lax.Precision.HIGHEST, preferred_element_type=F32,
        )

    known_ref[0] = spread(sums)
    known_ref[1] = jnp.zeros((LANES, LANES), F32)
    coarse_solve()
    gather_drain(ITERS)
    gather_drain(ITERS + 1)

    def iterate(turn, scalars):
        gamma, energy, alpha, beta = scalars
        parity = turn % 2
        own = known_ref[2, pl.ds(mine, 1), :]
        extra = jnp.where(row8 == 0, own * known_ref[0, pl.ds(mine, 1), :], 0.0)
        extra = jnp.where(row8 == 2, own * known_ref[1, pl.ds(mine, 1), :], extra)
        mode_sums = solve_lines(alpha, beta)

        def ends(t, carry):
            backward(parity, t * (size - PLANES), own)
            return carry

        def others(t, carry):
            backward(parity, t * PLANES, own)
            return carry

        lax.fori_loop(0, 2, ends, 0)
        halos = [halo_copy(turn, side) for side in range(4)]
        halos[0].start()
        halos[1].start()
        lax.fori_loop(1, size // PLANES - 1, others, 0)
        halos[2].start()
        halos[3].start()

        def apply_some(t, sums):
            for m in range(APPLIES):
                sums = apply(parity, APPLIES * t + m, sums)
            return sums

        zeros = (jnp.zeros((ROWS, LANES), F32),) * 2
        curve, flow = lax.fori_loop(0, size // APPLIES, apply_some, zeros)
        for halo in halos:
            halo.wait_recv()
        ghost = ghosts(turn)
        low = pl.ds(back_base(parity, 0), size)
        high = pl.ds(back_base(parity, size - 1), size)
        faces = [back_ref[low, :], back_ref[high, :], edge_ref[0], edge_ref[1]]
        for n in range(4):
            curve = curve - fold(faces[n] * ghost[n])
            flow = flow - fold(ghost[n])
        stacked = jnp.zeros((ROWS, LANES), F32)
        for n, total in enumerate((mode_sums[0], curve, mode_sums[1], flow)):
            stacked = jnp.where(row8 == n, jnp.sum(total, axis=0, keepdims=True), stacked)
        stacked = jnp.sum(stacked, axis=1, keepdims=True) + extra
        payload = jnp.sum(jnp.where(row8 == lane8, stacked, 0.0), axis=0, keepdims=True)
        gather_start(turn, payload)

        base = image_base(parity, 0)
        spots = [
            pl.ds(base, size), pl.ds(base + (size - 1) * size, size),
            pl.ds(base, size, stride=size), pl.ds(base + size - 1, size, stride=size),
        ]
        for n in range(4):
            image_ref[spots[n], :] = image_ref[spots[n], :] - ghost[n]

        @pl.when(turn < ITERS - 1)
        def _():
            forward_y(image_ref, parity)

        gather_middle(turn)

        @pl.when(turn < ITERS - 1)
        def _():
            forward_x()

        @pl.when(turn > 0)
        def _():
            update(1 - parity, alpha, beta)

        for halo in halos:
            halo.wait_send()
        every = gather_end(turn)
        totals = jnp.sum(every, axis=0, keepdims=True)
        fresh = lane_pick(totals, 0)
        beta = jnp.where(turn == 0, 0.0, fresh / gamma)
        energy = lane_pick(totals, 1) + beta * (2.0 * lane_pick(totals, 2) + beta * energy)
        alpha = fresh / energy
        known_ref[1] = spread(every) + beta[:1] * known_ref[1]
        known_ref[0] = known_ref[0] - alpha[:1] * known_ref[1]
        coarse_solve()
        gather_drain(turn)
        return fresh, energy, alpha, beta

    one = jnp.ones((ROWS, LANES), F32)
    zero = jnp.zeros((ROWS, LANES), F32)
    gamma, energy, alpha, beta = lax.fori_loop(0, ITERS, iterate, (one, zero, -one, zero))
    update((ITERS - 1) % 2, alpha, beta)


def shards(n_gx, n_gy, right_side, diagonal, sweep_counts, refine_flags, coarse_inverse):
    size, _, cells = right_side.shape
    flat = (size * size, cells)
    table = jnp.asarray(split_table(size))
    mu = jnp.asarray(np.repeat(eigen_values(size).astype(np.float32)[:, None], cells, axis=1))
    subs = n_gx * n_gy
    if coarse_inverse.shape[1] < LANES:
        coarse_inverse = jnp.pad(coarse_inverse, ((0, 0), (0, LANES - subs)))
    operands = (
        right_side.reshape(flat), diagonal.reshape(flat), sweep_counts, refine_flags, coarse_inverse, table, mu
    )
    vmem = pl.BlockSpec(memory_space=pltpu.VMEM)
    hbm = pl.BlockSpec(memory_space=pltpu.HBM)
    field = pltpu.VMEM(flat, F32)
    face = (size, LANES)
    outs = pl.pallas_call(
        functools.partial(kernel, n_gx, n_gy, size),
        out_shape=[jax.ShapeDtypeStruct(flat, F32)] * 2,
        in_specs=[hbm] * 7,
        out_specs=[vmem, vmem],
        scratch_shapes=[
            pltpu.SMEM(sweep_counts.shape, jnp.int32),
            pltpu.VMEM(refine_flags.shape, jnp.int32),
            pltpu.VMEM(coarse_inverse.shape, F32),
            pltpu.VMEM(table.shape, table.dtype),
            pltpu.VMEM(mu.shape, F32),
            field, field, field,
            pltpu.VMEM((2 * size * size, LANES), F32),
            pltpu.VMEM((2 * (size + 2) * (size + ROWS), LANES), F32),
            field, field, field, field,
            pltpu.VMEM((size * (size + 1), LANES), F32),
            pltpu.VMEM((size * (size + 1), LANES), F32),
            pltpu.VMEM((COLUMNS * size, LANES), F32),
            field, field, field, field,
            pltpu.VMEM((2,) + face, F32),
            pltpu.VMEM((ITERS, 2) + face, F32),
            pltpu.VMEM((ITERS, 2) + face, F32),
            pltpu.VMEM((GATHERS, n_gy, ROWS, LANES), F32),
            pltpu.VMEM((GATHERS, LANES // ROWS, ROWS, LANES), F32),
            pltpu.VMEM((3, LANES, LANES), F32),
            pltpu.SemaphoreType.DMA((7,)),
            pltpu.SemaphoreType.DMA((ITERS, 4)),
            pltpu.SemaphoreType.DMA((ITERS, 4)),
            pltpu.SemaphoreType.DMA((GATHERS, n_gy)),
            pltpu.SemaphoreType.DMA((GATHERS, n_gy)),
            pltpu.SemaphoreType.DMA((GATHERS, n_gx)),
            pltpu.SemaphoreType.DMA((GATHERS, n_gx)),
        ],
        compiler_params=pltpu.CompilerParams(
            collective_id=0, has_side_effects=True, vmem_limit_bytes=48 * 1024 * 1024
        ),
        cost_estimate=pl.CostEstimate(flops=4 * 10**9, bytes_accessed=8 * 2**20, transcendentals=0),
        name="pressure_solve",
    )(
        *(pltpu.with_memory_space_constraint(operand, pltpu.HBM) for operand in operands)
    )
    return tuple(out.reshape(right_side.shape) for out in outs)


def solution(mesh):
    return jax.shard_map(
        functools.partial(shards, mesh.shape["gx"], mesh.shape["gy"]),
        mesh=mesh,
        in_specs=(P("gx", "gy", None), P("gx", "gy", None), P(), P(), P(("gx", "gy"), None)),
        out_specs=(P("gx", "gy", None), P("gx", "gy", None)),
        check_vma=False,
    )
```

time: 120 us -> 114 us (0.950)
  Pallas kernels: 116 us -> 111 us
    pallas_call x1, Pallas kernels: 116 us -> 111 us  [shards(): pl.pallas_call(functools.partial(kernel, n_gx, n_gy, size), out_shape=[ja...]
where the time goes in v3:
time: 114 us
  Pallas kernels  111 us (97%)
  local copies, waits for them, and re-layouts  2.64 us (2%)
    pallas_call x1, Pallas kernels, shards(): pl.pallas_call(functools.partial(kernel, n_gx, n_gy, size), out_shape=[ja...  111 us
    unnamed x2, local copies, waits for them, and re-layouts  2.64 us

profile of v3, /device:TPU:1, one launch (start us, length us, event | category | flops | bytes accessed | tf_op | source)
XLA Modules:
  0.0 114.4 jit_solution(12567828582709152976)
XLA Ops:
  0.6 111.1 %pressure_solve.1 = (f32[4096,128]{1,0:T(8,128)S(1)}, f32[4096,128]{1,0:T(8,128)S(1)}) custom-call(f32[4096,128]{1,0:T(8,128)} %bitcast.6, f32[4096,128]{1,0:T(8,128)} %bitcast.7, s32[128]{0:T(128)} %count_hbm.1, s32[128,128]{1,0:T(8,128)} %flag_hbm.1, f32[1,128]{1,0:T(1,128)} %coarse_hbm.1, bf16[128,128]{1,0:T(8,128)(2,1)} %constant.4.clone.table_hbm, ...), custom_call_target="tpu_custom_call" | custom-call | flops 4000000000 | bytes 8388608 | tf_op jit(solution)/shard_map/pressure_solve/pallas_call | solution.py:492
  111.8 1.3 %copy.11 = f32[64,64,128]{2,1,0:T(8,128)} copy(f32[64,64,128]{2,1,0:T(8,128)S(1)} %bitcast.5) | data formatting | bytes 4194304
  113.1 1.3 %copy.12 = f32[64,64,128]{2,1,0:T(8,128)} copy(f32[64,64,128]{2,1,0:T(8,128)S(1)} %bitcast.4) | data formatting | bytes 4194304

commit v4 on v3

--- a/solution.py
+++ b/solution.py
@@ -39,15 +39,14 @@
     table = sine_table(count).astype(np.float32)
     high = table.astype(ml_dtypes.bfloat16)
     low = (table - high.astype(np.float32)).astype(ml_dtypes.bfloat16)
-    return np.concatenate([np.concatenate([high, high], axis=1), np.concatenate([low, low], axis=1)], axis=0)
+    return np.concatenate([high, high, low, low], axis=1)
 
 
 def transform(table, field):
     high = field.astype(jnp.bfloat16)
     low = (field - high.astype(F32)).astype(jnp.bfloat16)
-    stacked = jnp.concatenate([high, low], axis=0)
-    both = jnp.dot(table, stacked, preferred_element_type=F32)
-    return both[:field.shape[0]] + both[field.shape[0]:]
+    stacked = jnp.concatenate([high, low, high, low], axis=0)
+    return jnp.dot(table, stacked, preferred_element_type=F32)
 
 
 def fold(value):
@@ -186,13 +185,6 @@
         far_ref[plane(b), :] = near * pltpu.roll(near, 1, 1)
         mid_ref[plane(b), :] = square + pltpu.roll(square, LANES - 1, 1)
 
-    def coefficient_some(t, carry):
-        for m in range(4):
-            coefficients(4 * t + m)
-        return carry
-
-    lax.fori_loop(0, size // 4, coefficient_some, 0)
-
     def wipe(t, carry):
         here = pl.ds(pl.multiple_of(t * (4 * size), ROWS), 4 * size)
         for field in (p_ref, s_ref, x_ref, hat_s_ref, hat_r_ref):
@@ -212,8 +204,6 @@
         return carry
 
     lax.fori_loop(0, size, clear, 0)
-    gather_middle(ITERS)
-    gather_middle(ITERS + 1)
 
     count = jnp.full((ROWS, LANES), count_ref[mine], jnp.int32)
     count = jnp.concatenate([count] * (size // ROWS), axis=0)
@@ -231,27 +221,25 @@
     def odd_base(first):
         return pl.multiple_of(first * odd_pitch, ROWS)
 
-    def forward_y(source, parity):
-        def body(t, carry):
+    def forward_y(source, parity, also=None):
+        def body(t):
             base = image_base(parity, t * PLANES)
             target = odd_base(t * PLANES)
             parts = [source[rows(base, m), :] for m in range(PLANES)]
             for m, part in enumerate(transform_all(parts)):
                 step_ref[pl.ds(target + m * odd_pitch, size), :] = part
-            return carry
-
-        lax.fori_loop(0, size // PLANES, body, 0)
-
-    def forward_x():
-        def body(t, carry):
-            first = t * COLUMNS
-            base = pl.multiple_of(first * size, ROWS)
-            parts = [step_ref[pl.ds(first + m, size, stride=odd_pitch), :] for m in range(COLUMNS)]
-            for m, part in enumerate(transform_all(parts)):
-                hat_ref[rows(base, m), :] = part
-            return carry
-
-        lax.fori_loop(0, size // COLUMNS, body, 0)
+            if also is not None:
+                for m in range(PLANES):
+                    also(t * PLANES + m)
+
+        over(0, size // PLANES, body)
+
+    def forward_x(t):
+        first = t * COLUMNS
+        base = pl.multiple_of(first * size, ROWS)
+        parts = [step_ref[pl.ds(first + m, size, stride=odd_pitch), :] for m in range(COLUMNS)]
+        for m, part in enumerate(transform_all(parts)):
+            hat_ref[rows(base, m), :] = part
 
     def lines_sweep(base, shift, alpha, beta, sums):
         sums = list(sums)
@@ -348,7 +336,7 @@
         alpha = jnp.broadcast_to(alpha[:1], (size, LANES))
         beta = jnp.broadcast_to(beta[:1], (size, LANES))
 
-        def body(t, carry):
+        def body(t):
             base = pl.multiple_of(t * (UPDATES * size), ROWS)
             image = image_base(parity, t * UPDATES)
             back = back_base(parity, t * UPDATES)
@@ -360,12 +348,13 @@
                 p_ref[here, :] = direction
                 x_ref[here, :] = x_ref[here, :] + alpha * direction
                 r_ref[here, :] = r_ref[here, :] - alpha * moved
-            return carry
-
-        lax.fori_loop(0, size // UPDATES, body, 0)
-
-    forward_y(r_ref, 0)
-    forward_x()
+
+        return body
+
+    forward_y(r_ref, 0, coefficients)
+    gather_middle(ITERS)
+    gather_middle(ITERS + 1)
+    over(0, size // COLUMNS, forward_x)
     loads[6].wait()
     gather_end(ITERS)
     sums = gather_end(ITERS + 1)
@@ -446,13 +435,23 @@
 
         gather_middle(turn)
 
-        @pl.when(turn < ITERS - 1)
+        updated = update(1 - parity, alpha, beta)
+
+        def both(t):
+            forward_x(t)
+            updated(t)
+
+        @pl.when(turn == 0)
         def _():
-            forward_x()
-
-        @pl.when(turn > 0)
+            over(0, size // COLUMNS, forward_x)
+
+        @pl.when((turn > 0) & (turn < ITERS - 1))
         def _():
-            update(1 - parity, alpha, beta)
+            over(0, size // COLUMNS, both)
+
+        @pl.when(turn == ITERS - 1)
+        def _():
+            over(0, size // UPDATES, updated)
 
         for halo in halos:
             halo.wait_send()
@@ -471,7 +470,7 @@
     one = jnp.ones((ROWS, LANES), F32)
     zero = jnp.zeros((ROWS, LANES), F32)
     gamma, energy, alpha, beta = lax.fori_loop(0, ITERS, iterate, (one, zero, -one, zero))
-    update((ITERS - 1) % 2, alpha, beta)
+    over(0, size // UPDATES, update((ITERS - 1) % 2, alpha, beta))
 
 
 def shards(n_gx, n_gy, right_side, diagonal, sweep_counts, refine_flags, coarse_inverse):

time: 114 us -> 115 us (level)
  no operation moved by 1% of the time
where the time goes in v4:
time: 115 us
  Pallas kernels  112 us (97%)
  local copies, waits for them, and re-layouts  2.64 us (2%)
    pallas_call x1, Pallas kernels, shards(): pl.pallas_call(functools.partial(kernel, n_gx, n_gy, size), out_shape=[ja...  112 us
    unnamed x2, local copies, waits for them, and re-layouts  2.64 us

profile of v4, /device:TPU:1, one launch (start us, length us, event | category | flops | bytes accessed | tf_op | source)
XLA Modules:
  0.0 115.2 jit_solution(12406105530189068054)
XLA Ops:
  0.6 111.9 %pressure_solve.1 = (f32[4096,128]{1,0:T(8,128)S(1)}, f32[4096,128]{1,0:T(8,128)S(1)}) custom-call(f32[4096,128]{1,0:T(8,128)} %bitcast.6, f32[4096,128]{1,0:T(8,128)} %bitcast.7, s32[128]{0:T(128)} %count_hbm.1, s32[128,128]{1,0:T(8,128)} %flag_hbm.1, f32[1,128]{1,0:T(1,128)} %coarse_hbm.1, bf16[64,256]{1,0:T(8,128)(2,1)} %constant.4.clone.table_hbm, ...), custom_call_target="tpu_custom_call" | custom-call | flops 4000000000 | bytes 8388608 | tf_op jit(solution)/shard_map/pressure_solve/pallas_call | solution.py:491
  112.5 1.3 %copy.11 = f32[64,64,128]{2,1,0:T(8,128)} copy(f32[64,64,128]{2,1,0:T(8,128)S(1)} %bitcast.5) | data formatting | bytes 4194304
  113.9 1.3 %copy.12 = f32[64,64,128]{2,1,0:T(8,128)} copy(f32[64,64,128]{2,1,0:T(8,128)S(1)} %bitcast.4) | data formatting | bytes 4194304

commit v5 on v4

--- a/solution.py
+++ b/solution.py
@@ -54,14 +54,14 @@
 
 
 def kernel(
-    n_gx, n_gy, size,
+    n_gx, n_gy, inner, size,
     rhs_hbm, diag_hbm, count_hbm, flag_hbm, coarse_hbm, table_hbm, mu_hbm,
     x_ref, r_ref,
     count_ref, flag_ref, coarse_ref, table_ref, mu_ref,
     diag_ref, p_ref, s_ref, image_ref, back_ref, hat_ref, hat_s_ref, hat_r_ref, line_ref, step_ref, mode_ref,
     twice_ref, root_ref, near_ref, far_ref, mid_ref,
     edge_ref, ghost_x, ghost_y, small_ref, all_ref, known_ref,
-    in_sem, halo_send, halo_recv, row_send, row_recv, col_send, col_recv,
+    in_sem, halo_send, halo_recv, row_send, row_recv, col_send, col_recv, far_send, far_recv,
 ):
     gx = lax.axis_index("gx")
     gy = lax.axis_index("gy")
@@ -118,6 +118,9 @@
     over(1, n_gy, lambda step: greet(beside_row(step)))
     over(1, n_gx, lambda step: greet(beside_col(step)))
 
+    near_gx = lax.rem(gx, inner)
+    first_gx = gx - near_gx
+
     def row_copy(slot, step):
         return pltpu.make_async_remote_copy(
             src_ref=small_ref.at[slot, gy], dst_ref=small_ref.at[slot, gy],
@@ -129,28 +132,54 @@
         return pltpu.make_async_remote_copy(
             src_ref=all_ref.at[slot, gx], dst_ref=all_ref.at[slot, gx],
             send_sem=col_send.at[slot, step], recv_sem=col_recv.at[slot, step],
-            device_id=beside_col(step), device_id_type=MESH,
+            device_id=(first_gx + lax.rem(near_gx + step, inner), gy), device_id_type=MESH,
         )
+
+    def far_copy(slot, step):
+        block = all_ref.at[slot, pl.ds(first_gx, inner)]
+        return pltpu.make_async_remote_copy(
+            src_ref=block, dst_ref=block,
+            send_sem=far_send.at[slot, step], recv_sem=far_recv.at[slot, step],
+            device_id=beside_col(step * inner), device_id_type=MESH,
+        )
+
+    row_steps = range(1, n_gy)
+    col_steps = range(1, inner)
+    far_steps = range(1, n_gx // inner)
 
     def gather_start(slot, payload):
         small_ref[slot, gy] = jnp.where(row8 == gy, payload, 0.0)
-        over(1, n_gy, lambda step: row_copy(slot, step).start())
+        for step in row_steps:
+            row_copy(slot, step).start()
 
     def gather_middle(slot):
-        over(1, n_gy, lambda step: row_copy(slot, step).wait_recv())
+        for step in row_steps:
+            row_copy(slot, step).wait_recv()
         total = small_ref[slot, 0]
         for other in range(1, n_gy):
             total = total + small_ref[slot, other]
         all_ref[slot, gx] = total
-        over(1, n_gx, lambda step: col_copy(slot, step).start())
+        for step in col_steps:
+            col_copy(slot, step).start()
+
+    def gather_far(slot):
+        for step in col_steps:
+            col_copy(slot, step).wait_recv()
+        for step in far_steps:
+            far_copy(slot, step).start()
 
     def gather_end(slot):
-        over(1, n_gx, lambda step: col_copy(slot, step).wait_recv())
+        for step in far_steps:
+            far_copy(slot, step).wait_recv()
         return all_ref[slot].reshape(LANES, LANES)
 
     def gather_drain(slot):
-        over(1, n_gy, lambda step: row_copy(slot, step).wait_send())
-        over(1, n_gx, lambda step: col_copy(slot, step).wait_send())
+        for step in row_steps:
+            row_copy(slot, step).wait_send()
+        for step in col_steps:
+            col_copy(slot, step).wait_send()
+        for step in far_steps:
+            far_copy(slot, step).wait_send()
 
     def lane_pick(row, which):
         total = jnp.sum(jnp.where(slim == which, row, 0.0), axis=1, keepdims=True)
@@ -351,9 +380,11 @@
 
         return body
 
-    forward_y(r_ref, 0, coefficients)
     gather_middle(ITERS)
     gather_middle(ITERS + 1)
+    forward_y(r_ref, 0, coefficients)
+    gather_far(ITERS)
+    gather_far(ITERS + 1)
     over(0, size // COLUMNS, forward_x)
     loads[6].wait()
     gather_end(ITERS)
@@ -435,23 +466,15 @@
 
         gather_middle(turn)
 
-        updated = update(1 - parity, alpha, beta)
-
-        def both(t):
-            forward_x(t)
-            updated(t)
-
-        @pl.when(turn == 0)
+        @pl.when(turn < ITERS - 1)
         def _():
             over(0, size // COLUMNS, forward_x)
 
-        @pl.when((turn > 0) & (turn < ITERS - 1))
+        gather_far(turn)
+
+        @pl.when(turn > 0)
         def _():
-            over(0, size // COLUMNS, both)
-
-        @pl.when(turn == ITERS - 1)
-        def _():
-            over(0, size // UPDATES, updated)
+            over(0, size // UPDATES, update(1 - parity, alpha, beta))
 
         for halo in halos:
             halo.wait_send()
@@ -479,6 +502,7 @@
     table = jnp.asarray(split_table(size))
     mu = jnp.asarray(np.repeat(eigen_values(size).astype(np.float32)[:, None], cells, axis=1))
     subs = n_gx * n_gy
+    inner = 4 if n_gx % 4 == 0 and n_gx > 4 else 2
     if coarse_inverse.shape[1] < LANES:
         coarse_inverse = jnp.pad(coarse_inverse, ((0, 0), (0, LANES - subs)))
     operands = (
@@ -489,7 +513,7 @@
     field = pltpu.VMEM(flat, F32)
     face = (size, LANES)
     outs = pl.pallas_call(
-        functools.partial(kernel, n_gx, n_gy, size),
+        functools.partial(kernel, n_gx, n_gy, inner, size),
         out_shape=[jax.ShapeDtypeStruct(flat, F32)] * 2,
         in_specs=[hbm] * 7,
         out_specs=[vmem, vmem],
@@ -518,8 +542,10 @@
             pltpu.SemaphoreType.DMA((ITERS, 4)),
             pltpu.SemaphoreType.DMA((GATHERS, n_gy)),
             pltpu.SemaphoreType.DMA((GATHERS, n_gy)),
-            pltpu.SemaphoreType.DMA((GATHERS, n_gx)),
-            pltpu.SemaphoreType.DMA((GATHERS, n_gx)),
+            pltpu.SemaphoreType.DMA((GATHERS, inner)),
+            pltpu.SemaphoreType.DMA((GATHERS, inner)),
+            pltpu.SemaphoreType.DMA((GATHERS, n_gx // inner)),
+            pltpu.SemaphoreType.DMA((GATHERS, n_gx // inner)),
         ],
         compiler_params=pltpu.CompilerParams(
             collective_id=0, has_side_effects=True, vmem_limit_bytes=48 * 1024 * 1024

time: 115 us -> 124 us (1.078)
  Pallas kernels: 112 us -> 120 us
    pallas_call x1, Pallas kernels: 112 us -> 120 us  [shards(): pl.pallas_call(functools.partial(kernel, n_gx, n_gy, inner, size), out_sh...]
where the time goes in v5:
time: 124 us; the launch traced here: 123 us
  Pallas kernels  120 us (97%)
  local copies, waits for them, and re-layouts  2.64 us (2%)
    pallas_call x1, Pallas kernels, shards(): pl.pallas_call(functools.partial(kernel, n_gx, n_gy, inner, size), out_sh...  120 us
    unnamed x2, local copies, waits for them, and re-layouts  2.64 us

profile of v5, /device:TPU:1, one launch (start us, length us, event | category | flops | bytes accessed | tf_op | source)
XLA Modules:
  0.0 123.4 jit_solution(11760578336554588250)
XLA Ops:
  0.6 120.1 %pressure_solve.1 = (f32[4096,128]{1,0:T(8,128)S(1)}, f32[4096,128]{1,0:T(8,128)S(1)}) custom-call(f32[4096,128]{1,0:T(8,128)} %bitcast.6, f32[4096,128]{1,0:T(8,128)} %bitcast.7, s32[128]{0:T(128)} %count_hbm.1, s32[128,128]{1,0:T(8,128)} %flag_hbm.1, f32[1,128]{1,0:T(1,128)} %coarse_hbm.1, bf16[64,256]{1,0:T(8,128)(2,1)} %constant.4.clone.table_hbm, ...), custom_call_target="tpu_custom_call" | custom-call | flops 4000000000 | bytes 8388608 | tf_op jit(solution)/shard_map/pressure_solve/pallas_call | solution.py:515
  120.7 1.3 %copy.11 = f32[64,64,128]{2,1,0:T(8,128)} copy(f32[64,64,128]{2,1,0:T(8,128)S(1)} %bitcast.5) | data formatting | bytes 4194304
  122.0 1.3 %copy.12 = f32[64,64,128]{2,1,0:T(8,128)} copy(f32[64,64,128]{2,1,0:T(8,128)S(1)} %bitcast.4) | data formatting | bytes 4194304

commit v6 on v3

--- a/solution.py
+++ b/solution.py
@@ -15,7 +15,7 @@
 ROWS = 8
 GATHERS = ITERS + 2
 SUM_LANE = 3
-LINES = 4
+PAIRS = 2
 COLUMNS = 8
 PLANES = 16
 APPLIES = 8
@@ -60,7 +60,7 @@
     x_ref, r_ref,
     count_ref, flag_ref, coarse_ref, table_ref, mu_ref,
     diag_ref, p_ref, s_ref, image_ref, back_ref, hat_ref, hat_s_ref, hat_r_ref, line_ref, step_ref, mode_ref,
-    twice_ref, root_ref, near_ref, far_ref, mid_ref,
+    twice_ref, guess_ref, root_ref, near_ref, far_ref, mid_ref,
     edge_ref, ghost_x, ghost_y, small_ref, all_ref, known_ref,
     in_sem, halo_send, halo_recv, row_send, row_recv, col_send, col_recv,
 ):
@@ -175,23 +175,35 @@
 
     shift = 2.5 * flag_ref[pl.ds(mine, 1), :].astype(F32) + 2.5
 
-    def coefficients(b):
-        d = mu_ref[...] + mu_ref[pl.ds(b, 1), :] + shift
+    height = jnp.transpose(jnp.broadcast_to(shift, (LANES, LANES)))
+    two = 2 * size
+    wide_lane = lax.broadcasted_iota(jnp.int32, (LANES, LANES), 1)
+    wide_row = lax.broadcasted_iota(jnp.int32, (LANES, LANES), 0)
+
+    def turned(pair, offset=0):
+        return pl.ds(pl.multiple_of(pair * LANES, LANES) + offset, LANES)
+
+    def coefficients(pair):
+        columns = jnp.where(wide_lane < size, mu_ref[pl.ds(2 * pair, 1), :], mu_ref[pl.ds(2 * pair + 1, 1), :])
+        d = columns + mu_ref[pl.ds(size, 1), :] + height
         root = lax.rsqrt(d)
         root = root * (1.5 - 0.5 * d * root * root)
-        near = jnp.where(lane == 0, 0.0, root * pltpu.roll(root, 1, 1))
+        near = jnp.where(wide_row == 0, 0.0, root * pltpu.roll(root, 1, 0))
         square = near * near
-        root_ref[plane(b), :] = root
-        near_ref[plane(b), :] = near
-        far_ref[plane(b), :] = near * pltpu.roll(near, 1, 1)
-        mid_ref[plane(b), :] = square + pltpu.roll(square, LANES - 1, 1)
+        root_ref[turned(pair), :] = root
+        near_ref[turned(pair), :] = near
+        far_ref[turned(pair), :] = near * pltpu.roll(near, 1, 0)
+        mid_ref[turned(pair), :] = square + pltpu.roll(square, LANES - 1, 0)
 
     def coefficient_some(t, carry):
-        for m in range(4):
-            coefficients(4 * t + m)
+        coefficients(2 * t)
+        coefficients(2 * t + 1)
         return carry
 
     lax.fori_loop(0, size // 4, coefficient_some, 0)
+    near_ref[pl.ds(plain, ROWS), :] = jnp.zeros((ROWS, LANES), F32)
+    far_ref[pl.ds(plain, ROWS), :] = jnp.zeros((ROWS, LANES), F32)
+    guess_ref[...] = jnp.zeros_like(guess_ref)
 
     def wipe(t, carry):
         here = pl.ds(pl.multiple_of(t * (4 * size), ROWS), 4 * size)
@@ -216,7 +228,7 @@
     gather_middle(ITERS + 1)
 
     count = jnp.full((ROWS, LANES), count_ref[mine], jnp.int32)
-    count = jnp.concatenate([count] * (size // ROWS), axis=0)
+    count = jnp.concatenate([count] * (LANES // ROWS), axis=0)
     odd = count % 2 == 1
     active = [count > 2 * step for step in range(MOST // 2)]
 
@@ -253,34 +265,44 @@
 
         lax.fori_loop(0, size // COLUMNS, body, 0)
 
+    turn_over = jnp.transpose
+
     def lines_sweep(base, shift, alpha, beta, sums):
+        first = base
         sums = list(sums)
-        for part in range(0, COLUMNS, LINES):
-            here = [rows(base, m + part + shift) for m in range(LINES)]
-            kept = [pl.ds((part + m) * size, size) for m in range(LINES)]
+        for part in range(0, COLUMNS // 2, PAIRS):
+            pairs = range(part, part + PAIRS)
+            here = [pl.ds(base + n * two + shift * size, two) for n in pairs]
+            after = [[pl.ds(first + n * LANES + far, LANES) for far in range(3)] for n in pairs]
+            held = [n * (LANES + 2 * ROWS) + ROWS for n in pairs]
+            kept = [pl.ds(n * LANES, LANES) for n in pairs]
             guess = []
-            for m in range(LINES):
-                hat_s = hat_ref[here[m], :] + beta * hat_s_ref[here[m], :]
-                hat_r = hat_r_ref[here[m], :] - alpha * hat_s
-                hat_s_ref[here[m], :] = hat_s
-                hat_r_ref[here[m], :] = hat_r
-                near = near_ref[here[m], :]
-                start = hat_r * root_ref[here[m], :]
-                twice = start + near * pltpu.roll(start, 1, 1) + pltpu.roll(near * start, LANES - 1, 1)
-                twice_ref[kept[m], :] = twice
+            for n in range(PAIRS):
+                hat_s = hat_ref[here[n], :] + beta * hat_s_ref[here[n], :]
+                hat_r = hat_r_ref[here[n], :] - alpha * hat_s
+                hat_s_ref[here[n], :] = hat_s
+                hat_r_ref[here[n], :] = hat_r
+                start = turn_over(hat_r) * root_ref[after[n][0], :]
+                guess_ref[pl.ds(held[n], LANES), :] = start
+                low = guess_ref[pl.ds(held[n] - 1, LANES), :]
+                high = guess_ref[pl.ds(held[n] + 1, LANES), :]
+                twice = start + near_ref[after[n][0], :] * low + near_ref[after[n][1], :] * high
+                twice_ref[kept[n], :] = twice
                 guess.append(jnp.where(odd, start, twice))
             for step in range(1, MOST // 2):
-                for m in range(LINES):
-                    far = far_ref[here[m], :]
-                    fresh = (twice_ref[kept[m], :] + mid_ref[here[m], :] * guess[m]) + (
-                        far * pltpu.roll(guess[m], 2, 1) + pltpu.roll(far * guess[m], LANES - 2, 1)
+                for n in range(PAIRS):
+                    guess_ref[pl.ds(held[n], LANES), :] = guess[n]
+                    low = guess_ref[pl.ds(held[n] - 2, LANES), :]
+                    high = guess_ref[pl.ds(held[n] + 2, LANES), :]
+                    fresh = (twice_ref[kept[n], :] + mid_ref[after[n][0], :] * guess[n]) + (
+                        far_ref[after[n][0], :] * low + far_ref[after[n][2], :] * high
                     )
-                    guess[m] = jnp.where(active[step], fresh, guess[m])
-            for m in range(LINES):
-                line = guess[m] * root_ref[here[m], :]
-                line_ref[here[m], :] = line
-                sums[0] = sums[0] + fold(line * hat_r_ref[here[m], :])
-                sums[1] = sums[1] + fold(line * hat_s_ref[here[m], :])
+                    guess[n] = jnp.where(active[step], fresh, guess[n])
+            for n in range(PAIRS):
+                line = turn_over(guess[n] * root_ref[after[n][0], :])
+                line_ref[here[n], :] = line
+                sums[0] = sums[0] + fold(line * hat_r_ref[here[n], :])
+                sums[1] = sums[1] + fold(line * hat_s_ref[here[n], :])
         return tuple(sums)
 
     def lines_out(base, shift, target):
@@ -289,8 +311,8 @@
             mode_ref[pl.ds(target + m * odd_pitch, size), :] = part
 
     def solve_lines(alpha, beta):
-        alpha = jnp.broadcast_to(alpha[:1], (size, LANES))
-        beta = jnp.broadcast_to(beta[:1], (size, LANES))
+        alpha = jnp.broadcast_to(alpha[:1], (two, LANES))
+        beta = jnp.broadcast_to(beta[:1], (two, LANES))
 
         def body(t, sums):
             base = pl.multiple_of(t * (COLUMNS * size), ROWS)
@@ -478,7 +500,9 @@
     size, _, cells = right_side.shape
     flat = (size * size, cells)
     table = jnp.asarray(split_table(size))
-    mu = jnp.asarray(np.repeat(eigen_values(size).astype(np.float32)[:, None], cells, axis=1))
+    mu = eigen_values(size).astype(np.float32)
+    mu = np.concatenate([np.repeat(mu[:, None], cells, axis=1), np.tile(mu, (ROWS, cells // size))], axis=0)
+    mu = jnp.asarray(mu)
     subs = n_gx * n_gy
     if coarse_inverse.shape[1] < LANES:
         coarse_inverse = jnp.pad(coarse_inverse, ((0, 0), (0, LANES - subs)))
@@ -507,7 +531,11 @@
             pltpu.VMEM((size * (size + 1), LANES), F32),
             pltpu.VMEM((size * (size + 1), LANES), F32),
             pltpu.VMEM((COLUMNS * size, LANES), F32),
-            field, field, field, field,
+            pltpu.VMEM((COLUMNS // 2 * (LANES + 2 * ROWS), LANES), F32),
+            field,
+            pltpu.VMEM((size * size + ROWS, LANES), F32),
+            pltpu.VMEM((size * size + ROWS, LANES), F32),
+            field,
             pltpu.VMEM((2,) + face, F32),
             pltpu.VMEM((ITERS, 2) + face, F32),
             pltpu.VMEM((ITERS, 2) + face, F32),

time: 114 us -> 107 us (0.939)
  Pallas kernels: 111 us -> 104 us
    pallas_call x1, Pallas kernels: 111 us -> 104 us  [shards(): pl.pallas_call(functools.partial(kernel, n_gx, n_gy, size), out_shape=[ja...]
where the time goes in v6:
time: 107 us
  Pallas kernels  104 us (97%)
  local copies, waits for them, and re-layouts  2.64 us (2%)
    pallas_call x1, Pallas kernels, shards(): pl.pallas_call(functools.partial(kernel, n_gx, n_gy, size), out_shape=[ja...  104 us
    unnamed x2, local copies, waits for them, and re-layouts  2.64 us

profile of v6, /device:TPU:1, one launch (start us, length us, event | category | flops | bytes accessed | tf_op | source)
XLA Modules:
  0.0 107.0 jit_solution(12510245374810089722)
XLA Ops:
  0.6 103.8 %pressure_solve.1 = (f32[4096,128]{1,0:T(8,128)S(1)}, f32[4096,128]{1,0:T(8,128)S(1)}) custom-call(f32[4096,128]{1,0:T(8,128)} %bitcast.6, f32[4096,128]{1,0:T(8,128)} %bitcast.7, s32[128]{0:T(128)} %count_hbm.1, s32[128,128]{1,0:T(8,128)} %flag_hbm.1, f32[1,128]{1,0:T(1,128)} %coarse_hbm.1, bf16[128,128]{1,0:T(8,128)(2,1)} %constant.4.clone.table_hbm, ...), custom_call_target="tpu_custom_call" | custom-call | flops 4000000000 | bytes 8388608 | tf_op jit(solution)/shard_map/pressure_solve/pallas_call | solution.py:516
  104.4 1.3 %copy.11 = f32[64,64,128]{2,1,0:T(8,128)} copy(f32[64,64,128]{2,1,0:T(8,128)S(1)} %bitcast.5) | data formatting | bytes 4194304
  105.7 1.3 %copy.12 = f32[64,64,128]{2,1,0:T(8,128)} copy(f32[64,64,128]{2,1,0:T(8,128)S(1)} %bitcast.4) | data formatting | bytes 4194304

commit v7 on v6

--- a/solution.py
+++ b/solution.py
@@ -16,9 +16,9 @@
 GATHERS = ITERS + 2
 SUM_LANE = 3
 PAIRS = 2
-COLUMNS = 8
+COLUMNS = 16
 PLANES = 16
-APPLIES = 8
+APPLIES = 16
 UPDATES = 8
 F32 = jnp.float32
 MESH = pl.DeviceIdType.MESH

time: 107 us -> 107 us (level)
  no operation moved by 1% of the time
where the time goes in v7:
time: 107 us; the launch traced here: 106 us
  Pallas kernels  103 us (96%)
  local copies, waits for them, and re-layouts  2.64 us (2%)
    pallas_call x1, Pallas kernels, shards(): pl.pallas_call(functools.partial(kernel, n_gx, n_gy, size), out_shape=[ja...  103 us
    unnamed x2, local copies, waits for them, and re-layouts  2.64 us

profile of v7, /device:TPU:1, one launch (start us, length us, event | category | flops | bytes accessed | tf_op | source)
XLA Modules:
  0.0 106.4 jit_solution(15105635241948894587)
XLA Ops:
  0.6 103.1 %pressure_solve.1 = (f32[4096,128]{1,0:T(8,128)S(1)}, f32[4096,128]{1,0:T(8,128)S(1)}) custom-call(f32[4096,128]{1,0:T(8,128)} %bitcast.6, f32[4096,128]{1,0:T(8,128)} %bitcast.7, s32[128]{0:T(128)} %count_hbm.1, s32[128,128]{1,0:T(8,128)} %flag_hbm.1, f32[1,128]{1,0:T(1,128)} %coarse_hbm.1, bf16[128,128]{1,0:T(8,128)(2,1)} %constant.4.clone.table_hbm, ...), custom_call_target="tpu_custom_call" | custom-call | flops 4000000000 | bytes 8388608 | tf_op jit(solution)/shard_map/pressure_solve/pallas_call | solution.py:516
  103.8 1.3 %copy.11 = f32[64,64,128]{2,1,0:T(8,128)} copy(f32[64,64,128]{2,1,0:T(8,128)S(1)} %bitcast.5) | data formatting | bytes 4194304
  105.1 1.3 %copy.12 = f32[64,64,128]{2,1,0:T(8,128)} copy(f32[64,64,128]{2,1,0:T(8,128)S(1)} %bitcast.4) | data formatting | bytes 4194304

commit v8 on v7

--- a/solution.py
+++ b/solution.py
@@ -17,7 +17,7 @@
 SUM_LANE = 3
 PAIRS = 2
 COLUMNS = 16
-PLANES = 16
+PLANES = 32
 APPLIES = 16
 UPDATES = 8
 F32 = jnp.float32

time: 107 us -> 108 us (level)
    pallas_call x1, Pallas kernels: 103 us -> 104 us  [shards(): pl.pallas_call(functools.partial(kernel, n_gx, n_gy, size), out_shape=[ja...]
where the time goes in v8:
time: 108 us
  Pallas kernels  104 us (96%)
  local copies, waits for them, and re-layouts  2.64 us (2%)
    pallas_call x1, Pallas kernels, shards(): pl.pallas_call(functools.partial(kernel, n_gx, n_gy, size), out_shape=[ja...  104 us
    unnamed x2, local copies, waits for them, and re-layouts  2.64 us

profile of v8, /device:TPU:1, one launch (start us, length us, event | category | flops | bytes accessed | tf_op | source)
XLA Modules:
  0.0 107.5 jit_solution(3861263831175362390)
XLA Ops:
  0.6 104.3 %pressure_solve.1 = (f32[4096,128]{1,0:T(8,128)S(1)}, f32[4096,128]{1,0:T(8,128)S(1)}) custom-call(f32[4096,128]{1,0:T(8,128)} %bitcast.6, f32[4096,128]{1,0:T(8,128)} %bitcast.7, s32[128]{0:T(128)} %count_hbm.1, s32[128,128]{1,0:T(8,128)} %flag_hbm.1, f32[1,128]{1,0:T(1,128)} %coarse_hbm.1, bf16[128,128]{1,0:T(8,128)(2,1)} %constant.4.clone.table_hbm, ...), custom_call_target="tpu_custom_call" | custom-call | flops 4000000000 | bytes 8388608 | tf_op jit(solution)/shard_map/pressure_solve/pallas_call | solution.py:516
  104.9 1.3 %copy.11 = f32[64,64,128]{2,1,0:T(8,128)} copy(f32[64,64,128]{2,1,0:T(8,128)S(1)} %bitcast.5) | data formatting | bytes 4194304
  106.2 1.3 %copy.12 = f32[64,64,128]{2,1,0:T(8,128)} copy(f32[64,64,128]{2,1,0:T(8,128)S(1)} %bitcast.4) | data formatting | bytes 4194304
